TPU v7x, 128 devices: a whole 4x4x4 slice. The times are simulated.
128 devices in a mesh: tm: 8 (over z, x_hi), height: 16 (over y, x_lo, core).
Axes of the slice: x: 4 (x_hi: 2, x_lo: 2; x = x_hi * 2 + x_lo), y: 4, z: 4, core: 2. Of those that a mesh axis runs over, the one named last changes fastest.
Arguments:
- queries: bfloat16 [16, 16, 160, 2560], P('tm', 'height'), may hold values from -6 to 6
- keys: bfloat16 [16, 16, 160, 2560], P('tm', 'height'), may hold values from -6 to 6
- values: bfloat16 [16, 16, 160, 2560], P('tm', 'height'), may hold values from -6 to 6
- head_window_radius: int32 [20, 3], replicated, may hold values from 0 to 2, as said below
- output_weight: bfloat16 [2560, 2560], P('height'), may hold values from -0.125 to 0.125
- adapter_down_weight: bfloat16 [2560, 64], replicated, may hold values from -0.125 to 0.125
- adapter_up_weight: bfloat16 [64, 2560], replicated, may hold values from -0.75 to 0.75
- output_gradient: bfloat16 [16, 16, 160, 2560], P('tm', 'height'), may hold values from -6 to 6
Outputs:
- mixed: bfloat16 [16, 16, 160, 2560], P('tm', 'height')
- attention_gradient: bfloat16 [16, 16, 160, 2560], P('tm', 'height')
- grad_up: float32 [64, 2560], replicated
- grad_down: float32 [2560, 64], replicated
Inputs may be any that keep to these rules, and one draw needn't show every extreme that they name: `head_window_radius`: radii along frames and rows are 0 or 1, along columns 0 to 2; along each axis some head has the largest radius.
All inputs are finite; a program needn't handle non-finite values.
Results may differ from a plain program's by a relative error of at most 0.0063.
Values may be sent and summed in bfloat16 or wider, within the bound.
A program may use at most 128 MiB of HBM per device.

v0:
```python
import math

import jax
import jax.numpy as jnp
from jax import lax
from jax.sharding import PartitionSpec as P

HEADS = 20
HEAD_DIM = 128
TILE_W = 16


ADAPTER_SCALE = 2.0


def with_halo(cells, sides, width):
    for axis, dim in sides:
        count = lax.axis_size(axis)
        ends = count - 1
        head = lax.slice_in_dim(cells, 0, width, axis=dim)
        tail = lax.slice_in_dim(cells, cells.shape[dim] - width, cells.shape[dim], axis=dim)
        cells = jnp.concatenate(
            [
                lax.ppermute(tail, axis, [(i, (i + 1) % count) for i in range(ends)]),
                cells,
                lax.ppermute(head, axis, [((i + 1) % count, i) for i in range(ends)]),
            ],
            axis=dim,
        )
    return cells


def per_device(
    queries,
    keys,
    values,
    head_window_radius,
    output_weight,
    adapter_down_weight,
    adapter_up_weight,
    output_gradient,
):
    frames, row_total, column_count, feature_width = queries.shape
    out_width = output_gradient.shape[3]
    key_value = jnp.stack([keys, values])
    extended = with_halo(key_value, (("tm", 1), ("height", 2)), 1)
    frame_base = lax.axis_index("tm") * frames
    row_base = lax.axis_index("height") * row_total
    all_frames = frames * lax.axis_size("tm")
    all_rows = row_total * lax.axis_size("height")
    query_shape = (frames, row_total, column_count)
    key_shape = (frames + 2, row_total + 2, column_count)
    query_frame = jnp.broadcast_to(
        (frame_base + jnp.arange(frames, dtype=jnp.int32))[:, None, None], query_shape
    ).reshape(-1)
    query_row = jnp.broadcast_to(
        (row_base + jnp.arange(row_total, dtype=jnp.int32))[None, :, None], query_shape
    ).reshape(-1)
    query_tile = jnp.broadcast_to(
        (jnp.arange(column_count, dtype=jnp.int32) // TILE_W)[None, None, :], query_shape
    ).reshape(-1)
    key_frame = jnp.broadcast_to(
        (frame_base - 1 + jnp.arange(frames + 2, dtype=jnp.int32))[:, None, None], key_shape
    ).reshape(-1)
    key_row = jnp.broadcast_to(
        (row_base - 1 + jnp.arange(row_total + 2, dtype=jnp.int32))[None, :, None], key_shape
    ).reshape(-1)
    key_tile = jnp.broadcast_to(
        (jnp.arange(column_count, dtype=jnp.int32) // TILE_W)[None, None, :], key_shape
    ).reshape(-1)
    valid = (key_frame >= 0) & (key_frame < all_frames) & (key_row >= 0) & (key_row < all_rows)
    far_away = 1 << 20
    diff_frame = jnp.where(
        valid[None, :], jnp.abs(query_frame[:, None] - key_frame[None, :]), far_away
    )
    diff_row = jnp.abs(query_row[:, None] - key_row[None, :])
    diff_tile = jnp.abs(query_tile[:, None] - key_tile[None, :])
    token_count = frames * row_total * column_count
    query_flat = queries.reshape(token_count, feature_width)
    key_flat = extended[0].reshape(-1, feature_width)
    value_flat = extended[1].reshape(-1, feature_width)

    def one_head(head_index, attention_output):
        offset_first = head_index * HEAD_DIM
        query_head = lax.dynamic_slice_in_dim(query_flat, offset_first, HEAD_DIM, 1)
        key_head = lax.dynamic_slice_in_dim(key_flat, offset_first, HEAD_DIM, 1)
        value_head = lax.dynamic_slice_in_dim(value_flat, offset_first, HEAD_DIM, 1)
        scores = lax.dot_general(
            query_head, key_head, (((1,), (1,)), ((), ())), preferred_element_type=jnp.float32
        ) / math.sqrt(HEAD_DIM)
        radius = lax.dynamic_index_in_dim(head_window_radius, head_index, 0, keepdims=False)
        allowed = (diff_frame <= radius[0]) & (diff_row <= radius[1]) & (diff_tile <= radius[2])
        scores = jnp.where(allowed, scores, -1e30)
        highest = jnp.max(scores, axis=-1, keepdims=True)
        weights = jnp.exp(scores - highest)
        weights = (weights / jnp.sum(weights, axis=-1, keepdims=True)).astype(jnp.bfloat16)
        result = jnp.dot(weights, value_head, preferred_element_type=jnp.float32).astype(
            jnp.bfloat16
        )
        return lax.dynamic_update_slice_in_dim(attention_output, result, offset_first, 1)

    attention_output = lax.fori_loop(
        0, HEADS, one_head, jnp.zeros((token_count, feature_width), jnp.bfloat16)
    )
    output_cotangent = output_gradient.reshape(token_count, out_width)
    frozen_product = jnp.dot(
        attention_output,
        lax.all_gather(output_weight, "height", axis=0, tiled=True),
        preferred_element_type=jnp.float32,
    )
    frozen_backward = lax.dot_general(
        output_cotangent,
        lax.all_gather(output_weight, "height", axis=0, tiled=True),
        (((1,), (1,)), ((), ())),
        preferred_element_type=jnp.float32,
    )
    low_rank_product = jnp.dot(
        attention_output, adapter_down_weight, preferred_element_type=jnp.float32
    ).astype(jnp.bfloat16)
    mixed = frozen_product + ADAPTER_SCALE * jnp.dot(
        low_rank_product, adapter_up_weight, preferred_element_type=jnp.float32
    )
    low_rank_backward = lax.dot_general(
        output_cotangent,
        adapter_up_weight,
        (((1,), (1,)), ((), ())),
        preferred_element_type=jnp.float32,
    ).astype(jnp.bfloat16)
    attention_gradient = frozen_backward + ADAPTER_SCALE * lax.dot_general(
        low_rank_backward,
        adapter_down_weight,
        (((1,), (1,)), ((), ())),
        preferred_element_type=jnp.float32,
    )
    token_total = token_count * lax.axis_size("tm") * lax.axis_size("height")
    adapter_factor = ADAPTER_SCALE / math.sqrt(token_total)
    local_up = adapter_factor * lax.dot_general(
        low_rank_product,
        output_cotangent,
        (((0,), (0,)), ((), ())),
        preferred_element_type=jnp.float32,
    )
    local_down = adapter_factor * lax.dot_general(
        attention_output,
        low_rank_backward,
        (((0,), (0,)), ((), ())),
        preferred_element_type=jnp.float32,
    )
    grad_up, grad_down = lax.psum((local_up, local_down), ("tm", "height"))
    mixed = mixed.astype(jnp.bfloat16).reshape(frames, row_total, column_count, out_width)
    attention_gradient = attention_gradient.astype(jnp.bfloat16).reshape(
        frames, row_total, column_count, feature_width
    )
    return (mixed, attention_gradient, grad_up, grad_down)


def solution(mesh):
    in_specs = (
        P("tm", "height", None, None),
        P("tm", "height", None, None),
        P("tm", "height", None, None),
        P(),
        P("height", None),
        P(),
        P(),
        P("tm", "height", None, None),
    )
    out_specs = (P("tm", "height", None, None), P("tm", "height", None, None), P(), P())
    return jax.shard_map(
        per_device, mesh=mesh, in_specs=in_specs, out_specs=out_specs, check_vma=False
    )
```

profile of v0, /device:TPU:1, one launch (start us, length us, event | category | flops | bytes accessed | tf_op | source)
XLA Modules:
  0.0 648.5 jit_solution(18268813314230043277)
XLA Ops:
  8.1 2.3 fusion.22
  10.4 5.7 collective-permute-start
  16.1 1.3 collective-permute-start.1
  17.4 33.0 %collective-permute-done = bf16[2,1,1,160,2560]{4,3,1,2,0:T(8,128)(2,1)S(1)} collective-permute-done((bf16[2,1,1,160,2560]{4,3,1,2,0:T(8,128)(2,1)S(1)}, bf16[2,1,1,160,2560]{4,3,1,2,0:T(8,128)(2,1)S(1)}, u32[]{:S(2)}, u32[]{:S(2)}) %collective-permute-start) | collective-permute-done | bytes 1638432 | tf_op jit(solution)/shard_map/ppermute | solution.py:24
  50.5 37.4 %collective-permute-done.1 = bf16[2,1,1,160,2560]{4,3,1,2,0:T(8,128)(2,1)S(1)} collective-permute-done((bf16[2,1,1,160,2560]{4,3,1,2,0:T(8,128)(2,1)S(1)}, bf16[2,1,1,160,2560]{4,3,1,2,0:T(8,128)(2,1)S(1)}, u32[]{:S(2)}, u32[]{:S(2)}) %collective-permute-start.1) | collective-permute-done | bytes 1638432 | tf_op jit(solution)/shard_map/ppermute | solution.py:26
  87.9 3.5 pad_maximum_fusion.1
  91.4 4.5 collective-permute-start.2
  96.0 2.9 collective-permute-start.3
  100.1 1.7 convolution_convert_fusion
  101.8 126.7 %collective-permute-done.2 = bf16[2,4,1,160,2560]{4,3,1,2,0:T(8,128)(2,1)} collective-permute-done((bf16[2,4,1,160,2560]{4,3,1,2,0:T(8,128)(2,1)}, bf16[2,4,1,160,2560]{4,3,1,2,0:T(8,128)(2,1)}, u32[]{:S(2)}, u32[]{:S(2)}) %collective-permute-start.2) | collective-permute-done | bytes 6553632 | tf_op jit(solution)/shard_map/ppermute | solution.py:24
  228.4 71.9 %collective-permute-done.3 = bf16[2,4,1,160,2560]{4,3,1,2,0:T(8,128)(2,1)} collective-permute-done((bf16[2,4,1,160,2560]{4,3,1,2,0:T(8,128)(2,1)}, bf16[2,4,1,160,2560]{4,3,1,2,0:T(8,128)(2,1)}, u32[]{:S(2)}, u32[]{:S(2)}) %collective-permute-start.3) | collective-permute-done | bytes 6553632 | tf_op jit(solution)/shard_map/ppermute | solution.py:26
  300.4 9.2 %pad_maximum_fusion = bf16[2,4,3,160,2560]{4,3,1,2,0:T(8,128)(2,1)S(1)} fusion(bf16[2,4,1,160,2560]{4,3,1,2,0:T(8,128)(2,1)} %collective-permute-done.3, bf16[2,1,1,160,2560]{4,3,1,2,0:T(8,128)(2,1)} %copy-done.5, bf16[1,2,1,160,2560]{4,3,1,2,0:T(8,128)(2,1)S(1)} %bitcast.45, bf16[1,2,1,160,2560]{4,3,1,2,0:T(8,128)(2,1)S(1)} %bitcast.42, ...), kind=kLoop, calls=%fused_computation.22 | loop fusion | flops 49152000 | bytes 39321600 | tf_op jit(solution)/shard_map/concatenate | solution.py:22
  309.5 6.9 %fusion.27 = (bf16[1,4,3,160,2560]{4,3,1,2,0:T(8,128)(2,1)}, bf16[1,4,3,160,2560]{4,3,1,2,0:T(8,128)(2,1)}) fusion(bf16[2,4,3,160,2560]{4,3,1,2,0:T(8,128)(2,1)S(1)} %pad_maximum_fusion), kind=kLoop, calls=%fused_computation.53 | loop fusion | bytes 39321600 | tf_op jit(solution)/shard_map/slice | solution.py:81
  316.4 8.1 %copy.16 = bf16[1,4,3,160,2560]{4,3,2,1,0:T(8,128)(2,1)} copy(bf16[1,4,3,160,2560]{4,3,1,2,0:T(8,128)(2,1)} %get-tuple-element.233) | data formatting | bytes 19660800 | tf_op jit(solution)/shard_map/slice | solution.py:80
  324.6 8.1 %copy.17 = bf16[1,4,3,160,2560]{4,3,2,1,0:T(8,128)(2,1)} copy(bf16[1,4,3,160,2560]{4,3,1,2,0:T(8,128)(2,1)} %get-tuple-element.232) | data formatting | bytes 19660800 | tf_op jit(solution)/shard_map/slice | solution.py:81
  332.8 151.4 %while.14 = (s32[]{:T(128)}, bf16[320,2560]{1,0:T(8,128)(2,1)S(1)}, s32[20,3]{0,1:T(4,128)S(1)}, bf16[320,2560]{1,0:T(8,128)(2,1)}, bf16[1920,2560]{1,0:T(8,128)...) while((s32[]{:T(128)}, bf16[320,2560]{1,0:T(8,128)(2,1)S(1)}, ...), condition=%wide.region_3.4_spmd.clone, body=%wide.region_0.3_spmd.clone.sunk | while | flops 325059840 | bytes 8562299 | solution.py:102
  334.1 4.1 fusion.53
  338.7 1.7 fusion.55
  341.7 4.1 fusion.53
  346.3 1.7 fusion.55
  349.2 4.1 fusion.53
  353.9 1.7 fusion.55
  356.8 4.1 fusion.53
  361.4 1.7 fusion.55
  364.4 4.1 fusion.53
  369.0 1.7 fusion.55
  371.9 4.1 fusion.53
  376.6 1.7 fusion.55
  379.5 4.1 fusion.53
  384.1 1.7 fusion.55
  387.1 4.1 fusion.53
  391.7 1.7 fusion.55
  394.7 4.1 fusion.53
  399.3 1.7 fusion.55
  402.2 4.1 fusion.53
  406.9 1.7 fusion.55
  409.8 4.1 fusion.53
  414.4 1.7 fusion.55
  417.4 4.1 fusion.53
  422.0 1.7 fusion.55
  424.9 4.1 fusion.53
  429.6 1.7 fusion.55
  432.5 4.1 fusion.53
  437.1 1.7 fusion.55
  440.1 4.1 fusion.53
  444.7 1.7 fusion.55
  447.6 4.1 fusion.53
  452.3 1.7 fusion.55
  455.2 4.1 fusion.53
  459.9 1.7 fusion.55
  462.8 4.1 fusion.53
  467.4 1.7 fusion.55
  470.4 4.1 fusion.53
  475.0 1.7 fusion.55
  477.9 4.1 fusion.53
  482.6 1.7 fusion.55
  484.2 1.6 convolution_convert_fusion.1
  488.4 7.5 %fusion.28 = f32[320,2560]{1,0:T(8,128)S(1)} fusion(bf16[320,2560]{1,0:T(8,128)(2,1)S(1)} %get-tuple-element.158, bf16[2560,2560]{1,0:T(8,128)(2,1)} %all-gather.2.cloned.1.call-done), kind=kOutput, calls=%fused_computation.54 | convolution fusion | flops 4194304000 | bytes 18022400 | tf_op jit(solution)/shard_map/dot_general | solution.py:106
  495.9 7.7 %fusion.29 = f32[320,2560]{1,0:T(8,128)S(1)} fusion(bf16[320,2560]{1,0:T(8,128)(2,1)S(1)} %bitcast.37, bf16[2560,2560]{1,0:T(8,128)(2,1)} %all-gather.2.cloned.1.call-done), kind=kOutput, calls=%fused_computation.55 | convolution fusion | flops 4194304000 | bytes 18022400 | tf_op jit(solution)/shard_map/dot_general | solution.py:111
  503.6 1.8 fusion.20
  505.4 1.8 fusion.21
  507.2 129.9 %all-reduce.3.cloned.1.call-done = (f32[64,2560]{1,0:T(8,128)}, f32[2560,64]{0,1:T(8,128)}) async-done(((f32[64,2560]{1,0:T(8,128)}, f32[2560,64]{0,1:T(8,128)}), (f32[64,2560]{1,0:T(8,128)}, f32[2560,64]{0,1:T(8,128)})) %all-reduce.3.cloned.1.call-update) | async-done | bytes 1310736 | tf_op jit(solution)/shard_map/psum | solution.py:149
  637.1 2.0 copy.29
  639.0 2.0 copy.30
  (126 shorter events, 38.8 us)
Async XLA Ops:
  8.0 92.1 %copy-start = (bf16[2,1,160,2560]{3,2,1,0:T(8,128)(2,1)S(1)}, bf16[2,1,160,2560]{3,2,1,0:T(8,128)(2,1)}, u32[]{:S(2)}) copy-start(bf16[2,1,160,2560]{3,2,1,0:T(8,128)(2,1)} %param.17) | copy-start | bytes 4915204
  8.0 480.4 %all-gather.2.cloned.1.call-start = ((), (), s32[]{:S(2)}) async-start(), calls=%async_computation | async-start | bytes 13926400 | tf_op jit(solution)/shard_map/all_gather | solution.py:108
  8.1 79.8 %copy-start.1 = (bf16[2,1,160,2560]{3,2,1,0:T(8,128)(2,1)S(1)}, bf16[2,1,160,2560]{3,2,1,0:T(8,128)(2,1)}, u32[]{:S(2)}) copy-start(bf16[2,1,160,2560]{3,2,1,0:T(8,128)(2,1)} %param.11) | copy-start | bytes 4915204
  8.1 79.8 %copy-start.2 = (bf16[2,1,160,2560]{3,2,1,0:T(8,128)(2,1)S(1)}, bf16[2,1,160,2560]{3,2,1,0:T(8,128)(2,1)}, u32[]{:S(2)}) copy-start(bf16[2,1,160,2560]{3,2,1,0:T(8,128)(2,1)} %param.12) | copy-start | bytes 4915204
  10.4 40.1 %collective-permute-start = (bf16[2,1,1,160,2560]{4,3,1,2,0:T(8,128)(2,1)S(1)}, bf16[2,1,1,160,2560]{4,3,1,2,0:T(8,128)(2,1)S(1)}, u32[]{:S(2)}, u32[]{:S(2)}) collective-permute-start(bf16[2,1,1,160,2560]{4,3,1,2,0:T(8,128)(2,1)S(1)} %get-tuple-element.234), channel_id=1, source_target_pairs={{0,16},{16,32},{32,48},{48,64},{64,80},{80,96},{96,112},{1,17},{17... | collective-permute-start | bytes 4915208 | tf_op jit(solution)/shard_map/ppermute | solution.py:24
  16.1 71.8 %collective-permute-start.1 = (bf16[2,1,1,160,2560]{4,3,1,2,0:T(8,128)(2,1)S(1)}, bf16[2,1,1,160,2560]{4,3,1,2,0:T(8,128)(2,1)S(1)}, u32[]{:S(2)}, u32[]{:S(2)}) collective-permute-start(bf16[2,1,1,160,2560]{4,3,1,2,0:T(8,128)(2,1)S(1)} %get-tuple-element.235), channel_id=1, source_target_pairs={{16,0},{32,16},{48,32},{64,48},{80,64},{96,80},{112,96},{17,1},{33... | collective-permute-start | bytes 4915208 | tf_op jit(solution)/shard_map/ppermute | solution.py:26
  50.5 40.9 %copy-start.4 = (bf16[2,1,1,160,2560]{4,3,1,2,0:T(8,128)(2,1)}, bf16[2,1,1,160,2560]{4,3,1,2,0:T(8,128)(2,1)S(1)}, u32[]{:S(2)}) copy-start(bf16[2,1,1,160,2560]{4,3,1,2,0:T(8,128)(2,1)S(1)} %collective-permute-done) | copy-start | bytes 4915204
  87.9 3.5 copy-start.5
  91.4 137.0 %collective-permute-start.2 = (bf16[2,4,1,160,2560]{4,3,1,2,0:T(8,128)(2,1)}, bf16[2,4,1,160,2560]{4,3,1,2,0:T(8,128)(2,1)}, u32[]{:S(2)}, u32[]{:S(2)}) collective-permute-start(bf16[2,4,1,160,2560]{4,3,1,2,0:T(8,128)(2,1)} %pad_maximum_fusion.1), channel_id=1, source_target_pairs={{0,1},{1,2},{2,3},{3,4},{4,5},{5,6},{6,7},{7,8},{8,9},{9,10},{10,1... | collective-permute-start | bytes 19660808 | tf_op jit(solution)/shard_map/ppermute | solution.py:24
  96.0 204.4 %collective-permute-start.3 = (bf16[2,4,1,160,2560]{4,3,1,2,0:T(8,128)(2,1)}, bf16[2,4,1,160,2560]{4,3,1,2,0:T(8,128)(2,1)}, u32[]{:S(2)}, u32[]{:S(2)}) collective-permute-start(bf16[2,4,1,160,2560]{4,3,1,2,0:T(8,128)(2,1)} %pad_maximum_fusion.1), channel_id=1, source_target_pairs={{1,0},{2,1},{3,2},{4,3},{5,4},{6,5},{7,6},{8,7},{9,8},{10,9},{11,1... | collective-permute-start | bytes 19660808 | tf_op jit(solution)/shard_map/ppermute | solution.py:26
  98.9 538.2 %all-reduce.3.cloned.1.call-start = ((), (), s32[]{:S(2)}) async-start(), calls=%async_computation.1 | async-start | bytes 2621440 | tf_op jit(solution)/shard_map/psum | solution.py:149
  100.0 200.3 %copy-start.3 = (bf16[2,1,160,2560]{3,2,1,0:T(8,128)(2,1)S(1)}, bf16[2,1,160,2560]{3,2,1,0:T(8,128)(2,1)}, u32[]{:S(2)}) copy-start(bf16[2,1,160,2560]{3,2,1,0:T(8,128)(2,1)} %param.12) | copy-start | bytes 4915204
  324.6 8.2 %copy-start.8 = (s32[20,3]{0,1:T(4,128)S(1)}, s32[20,3]{0,1:T(4,128)}, u32[]{:S(2)}) copy-start(s32[20,3]{0,1:T(4,128)} %param.13) | copy-start | bytes 724
  495.9 7.7 %copy-start.6 = (bf16[64,2560]{1,0:T(8,128)(2,1)S(1)}, bf16[64,2560]{1,0:T(8,128)(2,1)}, u32[]{:S(2)}) copy-start(bf16[64,2560]{1,0:T(8,128)(2,1)} %param.16) | copy-start | bytes 983044
  503.6 1.8 copy-start.7
Sparse Core Ops, SparseCore 0:
  99.0 137.8 all-gather.1
Sparse Core Ops, SparseCore 1:
  488.5 148.5 all-reduce.2
where the time goes:
time: 651 us; the launch traced here: 648 us
  waiting for transfers between devices  399 us (61%)
  matrix products  140 us (22%)
  local copies, waits for them, and re-layouts  40.2 us (6%)
  other arithmetic  38 us (6%)
  between operations  15.7 us (2%)
  starting transfers between devices  14.5 us (2%)
    ppermute x2, waiting for transfers between devices, with_halo(): lax.ppermute(tail, axis, [(i, (i + 1) % count) for i in range(ends)])  160 us
    psum x1, waiting for transfers between devices, per_device(): grad_up, grad_down = lax.psum((local_up, local_down), ('tm', 'height'))  130 us
    ppermute x2, waiting for transfers between devices, with_halo(): lax.ppermute(head, axis, [((i + 1) % count, i) for i in range(ends)])  109 us
    dot_general x20, matrix products, one_head(): lax.dot_general(query_head, key_head, (((1,), (1,)), ((), ())), preferred...  82.6 us
    dot_general x20, matrix products, one_head(): jnp.dot(weights, value_head, preferred_element_type=jnp.float32)  33.1 us
    slice x2, local copies, waits for them, and re-layouts, per_device(): value_flat = extended[1].reshape(-1, feature_width)  15 us
  transfers between devices with their start and end apart: 6, of which 5 were waited for; matrix products, arithmetic and copies ran while one was open for 32% of the time, Pallas kernels for 0%

commit v1 on v0

v1 whole, which is shorter than its diff:
```python
import functools
import math

import jax
import jax.numpy as jnp
from jax import lax
from jax.experimental import pallas as pl
from jax.experimental.pallas import tpu as pltpu
from jax.sharding import PartitionSpec as P

HEADS = 20
HEAD_DIM = 128
TILE_W = 16
COLS = 160
HALF = COLS // 2
WINDOW = 128
RANK = 64
ADAPTER_SCALE = 2.0
GRID = 16
CHIPS = 4
GROUP_HEADS = HEADS // CHIPS
GROUP = GROUP_HEADS * HEAD_DIM
WIDTH = HEADS * HEAD_DIM
NEG = -1e30
MESH = pl.DeviceIdType.MESH
BF = jnp.bfloat16
F32 = jnp.float32


def place():
    tm, height = lax.axis_index("tm"), lax.axis_index("height")
    z, xh = tm // 2, tm % 2
    y, xl, core = height // 4, (height // 2) % 2, height % 2
    return z, xh, y, xl, core


def device(z, x, y, core):
    return (z * 2 + x // 2, y * 4 + (x % 2) * 2 + core)


def enter(partners):
    barrier = pltpu.get_barrier_semaphore()
    for partner in partners:
        pl.semaphore_signal(barrier, inc=1, device_id=partner, device_id_type=MESH)
    pl.semaphore_wait(barrier, len(partners))


def remote(src, dst, send, recv, target):
    return pltpu.make_async_remote_copy(
        src_ref=src, dst_ref=dst, send_sem=send, recv_sem=recv, device_id=target, device_id_type=MESH
    )


def arrived(dst, sem):
    pltpu.make_async_copy(dst, dst, sem).wait()


def group_columns(x):
    return pl.ds(pl.multiple_of(x * GROUP, 128), GROUP)


def spread_kernel(q_ref, k_ref, v_ref, qs_ref, ks_ref, vs_ref, out_sem, in_sem, halo_out, halo_in):
    z, xh, y, xl, core = place()
    x = xh * 2 + xl
    here = xl == core
    band = y * 2 + core
    before, after = (band + 7) % 8, (band + 1) % 8
    up, down = device((z + 3) % 4, x, y, core), device((z + 1) % 4, x, y, core)
    left = device(z, x, before // 2, before % 2)
    right = device(z, x, after // 2, after % 2)
    ring = x * 2 + core
    partners = []
    for step in range(1, 8):
        other = (ring + step) % 8
        partners.append(device(z, other // 2, y, other % 2))
    outside = (band + 7 + 2 * core) % 8
    partners += [up, down, device(z, x, outside // 2, outside % 2)]
    enter(partners)

    arrays = ((k_ref, ks_ref, 1), (v_ref, vs_ref, 1), (q_ref, qs_ref, 0))

    def exchange(i, step):
        src, dst, pad = arrays[i]
        target = (x + step) % CHIPS
        piece = src.at[:, 0, :, group_columns(target)]
        slot = dst.at[pl.ds(pad + 2 * xh, 2), pad + core]
        return piece, slot, remote(
            piece, slot, out_sem.at[i, step], in_sem.at[i, xh * 2 + core], device(z, target, y, xl)
        )

    for i in range(3):
        for step in (2, 1, 3):
            exchange(i, step)[2].start()
        piece, slot, copy = exchange(i, 0)

        @pl.when(here)
        def _():
            pltpu.make_async_copy(piece, slot, in_sem.at[i, xh * 2 + core]).start()

        @pl.when(jnp.logical_not(here))
        def _():
            copy.start()

    def landed(i):
        _, dst, pad = arrays[i]
        for source in range(4):
            arrived(dst.at[pl.ds(pad + 2 * (source // 2), 2), pad + source % 2], in_sem.at[i, source])

    def halos(i):
        ref = arrays[i][1]

        def send(n, src, dst, target):
            return remote(src, dst, halo_out.at[i, n], halo_in.at[i, n], target)

        rows = pl.ds(1, 2)
        own = pl.ds(1, 4)
        first = [
            send(0, ref.at[1, rows], ref.at[5, rows], up),
            send(1, ref.at[4, rows], ref.at[0, rows], down),
            send(2, ref.at[own, 1], ref.at[own, 3], left),
            send(3, ref.at[own, 2], ref.at[own, 0], right),
        ]
        second = [
            send(4, ref.at[0, 1], ref.at[0, 3], left),
            send(5, ref.at[5, 1], ref.at[5, 3], left),
            send(6, ref.at[0, 2], ref.at[0, 0], right),
            send(7, ref.at[5, 2], ref.at[5, 0], right),
        ]
        return first, second

    halo = [halos(0), halos(1)]
    for i in range(2):
        landed(i)
        for copy in halo[i][0]:
            copy.start()
    for i in range(2):
        halo[i][0][0].wait_recv()
        halo[i][0][1].wait_recv()
        for copy in halo[i][1]:
            copy.start()
    landed(2)
    for i in range(2):
        first, second = halo[i]
        for copy in first[2:] + second:
            copy.wait_recv()
        for copy in first + second:
            copy.wait_send()
    for i in range(3):
        for step in (2, 1, 3):
            exchange(i, step)[2].wait_send()
        copy = exchange(i, 0)[2]

        @pl.when(jnp.logical_not(here))
        def _():
            copy.wait_send()


def spread(queries, keys, values):
    any_space = pl.BlockSpec(memory_space=pl.ANY)
    halo_shape = jax.ShapeDtypeStruct((6, 4, COLS, GROUP), BF)
    return pl.pallas_call(
        spread_kernel,
        out_shape=(jax.ShapeDtypeStruct((4, 2, COLS, GROUP), BF), halo_shape, halo_shape),
        in_specs=[any_space] * 3,
        out_specs=(any_space,) * 3,
        scratch_shapes=[
            pltpu.SemaphoreType.DMA((3, 4)),
            pltpu.SemaphoreType.DMA((3, 4)),
            pltpu.SemaphoreType.DMA((2, 8)),
            pltpu.SemaphoreType.DMA((2, 8)),
        ],
        compiler_params=pltpu.CompilerParams(collective_id=0, has_side_effects=True),
        cost_estimate=pl.CostEstimate(flops=0, bytes_accessed=200_000_000, transcendentals=0),
        name="spread_heads",
    )(queries, keys, values)


def attention_kernel(radius_ref, q_ref, k_ref, v_ref, o_ref):
    z, xh, y, xl, core = place()
    head = (xh * 2 + xl) * GROUP_HEADS + pl.program_id(0)
    f = pl.program_id(1)
    frame = z * 4 + f
    row_first = y * 4 + core * 2
    radius_frame = radius_ref[head * 3]
    radius_row = radius_ref[head * 3 + 1]
    radius_column = radius_ref[head * 3 + 2]
    scale = math.log2(math.e) / math.sqrt(HEAD_DIM)

    def attend(reach_frame, reach_row):
        for half in range(2):
            start = (COLS - WINDOW) * half
            query_tile = (lax.broadcasted_iota(jnp.int32, (HALF, WINDOW), 0) + half * HALF) // TILE_W
            key_tile = (lax.broadcasted_iota(jnp.int32, (HALF, WINDOW), 1) + start) // TILE_W
            near = jnp.abs(query_tile - key_tile) <= radius_column
            for r in range(2):
                q = q_ref[0, r, pl.ds(half * HALF, HALF), :]
                scores, values = [], []
                for df in range(-reach_frame, reach_frame + 1):
                    for dr in range(-reach_row, reach_row + 1):
                        k = k_ref[f + 1 + df, r + 1 + dr, pl.ds(start, WINDOW), :]
                        values.append(v_ref[f + 1 + df, r + 1 + dr, pl.ds(start, WINDOW), :])
                        s = lax.dot_general(
                            q, k, (((1,), (1,)), ((), ())), preferred_element_type=F32
                        )
                        allowed = near
                        if df != 0 or dr != 0:
                            row = row_first + r + dr
                            inside = (
                                (frame + df >= 0) & (frame + df < GRID) & (row >= 0) & (row < GRID)
                            )
                            allowed = near & inside
                        scores.append(jnp.where(allowed, s, NEG))
                highest = functools.reduce(jnp.maximum, scores)
                highest = jnp.max(highest, axis=1, keepdims=True)
                weights = [jnp.exp2((s - highest) * scale) for s in scores]
                total = jnp.sum(functools.reduce(jnp.add, weights), axis=1, keepdims=True)
                weights = jnp.concatenate([w.astype(BF) for w in weights], axis=1)
                result = jnp.dot(
                    weights, jnp.concatenate(values, axis=0), preferred_element_type=F32
                )
                o_ref[0, r, pl.ds(half * HALF, HALF), :] = (result / total).astype(BF)

    for reach_frame in range(2):
        for reach_row in range(2):

            @pl.when((radius_frame == reach_frame) & (radius_row == reach_row))
            def _():
                attend(reach_frame, reach_row)


def attention(radius, qs, ks, vs):
    wide = pl.BlockSpec((6, 4, COLS, HEAD_DIM), lambda h, f, radius: (0, 0, 0, h))
    narrow = pl.BlockSpec((1, 2, COLS, HEAD_DIM), lambda h, f, radius: (f, 0, 0, h))
    return pl.pallas_call(
        attention_kernel,
        out_shape=jax.ShapeDtypeStruct((4, 2, COLS, GROUP), BF),
        grid_spec=pltpu.PrefetchScalarGridSpec(
            num_scalar_prefetch=1,
            grid=(GROUP_HEADS, 4),
            in_specs=[narrow, wide, wide],
            out_specs=narrow,
        ),
        compiler_params=pltpu.CompilerParams(vmem_limit_bytes=40 * 2**20),
        cost_estimate=pl.CostEstimate(
            flops=3_000_000_000, bytes_accessed=14_000_000, transcendentals=3_000_000
        ),
        name="attend",
    )(radius.reshape(-1), qs, ks, vs)


def finish_kernel(
    factor, o_ref, w_hbm, g_ref, down_ref, up_ref, mixed_ref, back_ref, grads_ref,
    w_ref, att_ref, part_ref, ra_ref, acc_ref, rb_ref, sum_ref, rc_ref, rd_ref, fin_ref,
    w_sem, o_out, o_in, a_out, a_in, b_out, b_in, c_out, c_in, d_out, d_in, e_out, e_in,
):
    z, xh, y, xl, core = place()
    x = xh * 2 + xl
    here = xl == core
    ring = x * 2 + core
    load = pltpu.make_async_copy(w_hbm, w_ref, w_sem)
    load.start()

    def ring_device(step):
        other = (ring + step) % 8
        return other // 2, other % 2, device(z, other // 2, y, other % 2)

    def y_device(step):
        return device(z, x, (y + step) % 4, core)

    def z_device(step):
        return device((z + step) % 4, x, y, core)

    enter(
        [ring_device(step)[2] for step in range(1, 8)]
        + [y_device(step) for step in range(1, 4)]
        + [z_device(step) for step in range(1, 4)]
    )

    def give_back(n):
        frames = (xh + n // 2) % 2
        row = (core + n % 2) % 2
        piece = o_ref.at[pl.ds(2 * frames, 2), row]
        slot = att_ref.at[:, :, group_columns(x)]
        return piece, slot, remote(
            piece, slot, o_out.at[n], o_in.at[x], device(z, frames * 2 + core, y, row)
        )

    for n in (2, 3, 1):
        give_back(n)[2].start()
    piece, slot, copy = give_back(0)

    @pl.when(here)
    def _():
        pltpu.make_async_copy(piece, slot, o_in.at[x]).start()

    @pl.when(jnp.logical_not(here))
    def _():
        copy.start()

    contract_last = (((1,), (1,)), ((), ()))
    contract_first = (((0,), (0,)), ((), ()))
    tokens = 2 * COLS
    gradient = g_ref[...].reshape(tokens, WIDTH)
    low_back = lax.dot_general(
        gradient, up_ref[...], contract_last, preferred_element_type=F32
    ).astype(BF)
    load.wait()
    step_width = 256

    def backward(j, carry):
        rows = pl.ds(pl.multiple_of(j * step_width, step_width), step_width)
        frozen = lax.dot_general(
            g_ref[...].reshape(tokens, WIDTH), w_ref[rows, :], contract_last, preferred_element_type=F32
        )
        adapter = lax.dot_general(
            low_back, down_ref[rows, :], contract_last, preferred_element_type=F32
        )
        back_ref[:, :, rows] = (
            (frozen + ADAPTER_SCALE * adapter).astype(BF).reshape(2, COLS, step_width)
        )
        return carry

    lax.fori_loop(0, WIDTH // step_width, backward, 0)

    for source in range(CHIPS):
        arrived(att_ref.at[:, :, pl.ds(source * GROUP, GROUP)], o_in.at[source])
    attended = att_ref[...].reshape(tokens, WIDTH)
    low = jnp.dot(attended, down_ref[...], preferred_element_type=F32).astype(BF)
    part_ref[0] = (
        factor * lax.dot_general(low, gradient, contract_first, preferred_element_type=F32)
    ).astype(BF)
    part_ref[1] = (
        factor * lax.dot_general(low_back, attended, contract_first, preferred_element_type=F32)
    ).astype(BF)

    def phase_a(step):
        tx, tc, target = ring_device(step)
        return remote(
            part_ref.at[tc, :, group_columns(tx)], ra_ref.at[step - 1],
            a_out.at[step - 1], a_in.at[step - 1], target,
        )

    for step in range(1, 8):
        phase_a(step).start()

    def forward(j, carry):
        columns = pl.ds(pl.multiple_of(j * step_width, step_width), step_width)
        frozen = jnp.dot(
            att_ref[...].reshape(tokens, WIDTH), w_ref[:, columns], preferred_element_type=F32
        )
        adapter = jnp.dot(low, up_ref[:, columns], preferred_element_type=F32)
        mixed_ref[:, :, columns] = (
            (frozen + ADAPTER_SCALE * adapter).astype(BF).reshape(2, COLS, step_width)
        )
        return carry

    lax.fori_loop(0, WIDTH // step_width, forward, 0)

    total = part_ref[core, :, group_columns(x)].astype(F32)
    for step in range(1, 8):
        phase_a(step).wait_recv()
        total = total + ra_ref[step - 1].astype(F32)
    acc_ref[...] = total

    def chunk(n):
        return pl.ds(pl.multiple_of(n * 16, 16), 16)

    def phase_b(step):
        return remote(
            acc_ref.at[chunk((y + step) % 4)], rb_ref.at[step - 1],
            b_out.at[step - 1], b_in.at[step - 1], y_device(step),
        )

    for step in range(1, 4):
        phase_b(step).start()
    total = acc_ref[chunk(y), :]
    for step in range(1, 4):
        phase_b(step).wait_recv()
        total = total + rb_ref[step - 1]
    sum_ref[...] = total

    def phase_c(step):
        return remote(
            sum_ref, rc_ref.at[step - 1], c_out.at[step - 1], c_in.at[step - 1], z_device(step)
        )

    for step in range(1, 4):
        phase_c(step).start()
    for step in range(1, 4):
        phase_c(step).wait_recv()

    total = jnp.zeros((16, GROUP), F32)
    for source in range(4):
        back = (z - source + 4) % 4
        term = sum_ref[...]
        for step in range(1, 4):
            term = jnp.where(back == step, rc_ref[step - 1], term)
        total = total + term
    rd_ref[chunk(y), :] = total.astype(BF)

    def phase_d(step):
        return remote(
            rd_ref.at[chunk(y)], rd_ref.at[chunk(y)],
            d_out.at[step - 1], d_in.at[step - 1], y_device(step),
        )

    for step in range(1, 4):
        phase_d(step).start()
    for step in range(1, 4):
        arrived(rd_ref.at[chunk((y - step + 4) % 4)], d_in.at[step - 1])

    def phase_e(step):
        return remote(
            rd_ref, fin_ref.at[core, :, group_columns(x)],
            e_out.at[step - 1], e_in.at[step - 1], ring_device(step)[2],
        )

    for step in range(1, 8):
        phase_e(step).start()
    fin_ref[core, :, group_columns(x)] = rd_ref[...]
    for step in range(1, 8):
        other = (ring - step + 8) % 8
        arrived(fin_ref.at[other % 2, :, group_columns(other // 2)], e_in.at[step - 1])
    grads_ref[...] = fin_ref[...].astype(F32)

    for n in (2, 3, 1):
        give_back(n)[2].wait_send()
    copy = give_back(0)[2]

    @pl.when(jnp.logical_not(here))
    def _():
        copy.wait_send()

    for step in range(1, 8):
        phase_a(step).wait_send()
        phase_e(step).wait_send()
    for step in range(1, 4):
        phase_b(step).wait_send()
        phase_c(step).wait_send()
        phase_d(step).wait_send()


def finish(factor, attended, weight, gradient, down, up):
    whole = pl.BlockSpec(memory_space=pltpu.VMEM)
    any_space = pl.BlockSpec(memory_space=pl.ANY)
    block = jax.ShapeDtypeStruct((2, COLS, WIDTH), BF)
    dma = pltpu.SemaphoreType.DMA
    return pl.pallas_call(
        functools.partial(finish_kernel, factor),
        out_shape=(block, block, jax.ShapeDtypeStruct((2, RANK, WIDTH), F32)),
        in_specs=[any_space, any_space, whole, whole, whole],
        out_specs=(whole,) * 3,
        scratch_shapes=[
            pltpu.VMEM((WIDTH, WIDTH), BF),
            pltpu.VMEM((2, COLS, WIDTH), BF),
            pltpu.VMEM((2, RANK, WIDTH), BF),
            pltpu.VMEM((7, RANK, GROUP), BF),
            pltpu.VMEM((RANK, GROUP), F32),
            pltpu.VMEM((3, 16, GROUP), F32),
            pltpu.VMEM((16, GROUP), F32),
            pltpu.VMEM((3, 16, GROUP), F32),
            pltpu.VMEM((RANK, GROUP), BF),
            pltpu.VMEM((2, RANK, WIDTH), BF),
            dma, dma((4,)), dma((4,)), dma((7,)), dma((7,)), dma((3,)), dma((3,)),
            dma((3,)), dma((3,)), dma((3,)), dma((3,)), dma((7,)), dma((7,)),
        ],
        compiler_params=pltpu.CompilerParams(
            collective_id=1, has_side_effects=True, vmem_limit_bytes=48 * 2**20
        ),
        cost_estimate=pl.CostEstimate(
            flops=9_000_000_000, bytes_accessed=100_000_000, transcendentals=0
        ),
        name="project_and_reduce",
    )(attended, weight, gradient, down, up)


def per_device(
    queries, keys, values, head_window_radius, output_weight, adapter_down_weight, adapter_up_weight,
    output_gradient,
):
    weight = lax.all_gather(output_weight, "height", axis=0, tiled=True)
    qs, ks, vs = spread(queries, keys, values)
    attended = attention(head_window_radius, qs, ks, vs)
    factor = ADAPTER_SCALE / math.sqrt(GRID * GRID * COLS)
    mixed, back, grads = finish(
        factor, attended, weight, output_gradient.reshape(2, COLS, WIDTH), adapter_down_weight,
        adapter_up_weight,
    )
    shape = (2, 1, COLS, WIDTH)
    return mixed.reshape(shape), back.reshape(shape), grads[0], grads[1].T


def solution(mesh):
    tokens = P("tm", "height", None, None)
    return jax.shard_map(
        per_device,
        mesh=mesh,
        in_specs=(tokens, tokens, tokens, P(), P("height", None), P(), P(), tokens),
        out_specs=(tokens, tokens, P(), P()),
        check_vma=False,
    )
```

time: 651 us -> 230 us (0.35)
  waiting for transfers between devices: 399 us -> 0.68 us
  Pallas kernels: 0 us -> 201 us
  matrix products: 140 us -> 0 us
  other arithmetic: 38 us -> 0 us
  local copies, waits for them, and re-layouts: 40.2 us -> 13.2 us
  starting transfers between devices: 14.5 us -> 0.04 us
    ppermute x4 -> x0, waiting for transfers between devices: 269 us -> none  [the longest x2 160 us: with_halo(): lax.ppermute(tail, axis, [(i, (i + 1) % count) for i in range(ends)])]
    pallas_call x0 -> x3, Pallas kernels: none -> 201 us  [the longest x1 109 us: spread(): pl.pallas_call(spread_kernel, out_shape=(jax.ShapeDtypeStruct((4, 2, COLS...]
    dot_general x48 -> x0, matrix products: 140 us -> none  [the longest x20 82.6 us: one_head(): lax.dot_general(query_head, key_head, (((1,), (1,)), ((), ())), preferred...]
    psum x1 -> x0, waiting for transfers between devices: 130 us -> none  [per_device(): grad_up, grad_down = lax.psum((local_up, local_down), ('tm', 'height'))]
    slice x23 -> x0, local copies, waits for them, and re-layouts: 33.6 us -> none  [the longest x2 15 us: per_device(): value_flat = extended[1].reshape(-1, feature_width)]
    ppermute x4 -> x0, starting transfers between devices: 14.5 us -> none  [the longest x2 10.3 us: with_halo(): lax.ppermute(tail, axis, [(i, (i + 1) % count) for i in range(ends)])]
    le x20 -> x0, other arithmetic: 13 us -> none  [one_head(): diff_row <= radius[1]]
    concatenate x2 -> x0, other arithmetic: 12.7 us -> none  [with_halo(): jnp.concatenate([lax.ppermute(tail, axis, [(i, (i + 1) % count) for i in...]
  transfers between devices with their start and end apart: 6 -> 1, of which waited for: 5 -> 0; matrix products, arithmetic and copies ran while one was open for 32% -> 1% of each run, Pallas kernels for 0% -> 61%
where the time goes in v1:
time: 230 us; the launch traced here: 229 us
  Pallas kernels  201 us (87%)
  between operations  14.1 us (6%)
  local copies, waits for them, and re-layouts  13.2 us (6%)
    pallas_call x1, Pallas kernels, spread(): pl.pallas_call(spread_kernel, out_shape=(jax.ShapeDtypeStruct((4, 2, COLS...  109 us
    pallas_call x1, Pallas kernels, finish(): pl.pallas_call(functools.partial(finish_kernel, factor), out_shape=(block...  61.4 us
    pallas_call x1, Pallas kernels, attention(): pl.pallas_call(attention_kernel, out_shape=jax.ShapeDtypeStruct((4, 2, CO...  30.8 us
    unnamed x14, local copies, waits for them, and re-layouts  11.9 us
  transfers between devices with their start and end apart: 1, of which 0 were waited for; matrix products, arithmetic and copies ran while one was open for 1% of the time, Pallas kernels for 61%

profile of v1, /device:TPU:1, one launch (start us, length us, event | category | flops | bytes accessed | tf_op | source)
XLA Modules:
  0.0 229.2 jit_solution(12005276177499144809)
XLA Ops:
  7.2 0.0 all-gather.2.cloned.1.call-start
  7.2 0.7 all-gather.2.cloned.1.call-update
  7.9 0.8 copy.16
  8.7 0.1 reshape.20.radius_ref
  8.8 1.3 copy.17.down_ref
  10.1 109.0 %spread_heads.1 = (bf16[4,2,160,640]{3,2,1,0:T(8,128)(2,1)}, bf16[6,4,160,640]{3,2,1,0:T(8,128)(2,1)}, bf16[6,4,160,640]{3,2,1,0:T(8,128)(2,1)}) custom-call(bf16[2,1,160,2560]{3,2,1,0:T(8,128)(2,1)} %q_ref.1, bf16[2,1,160,2560]{3,2,1,0:T(8,128)(2,1)} %k_ref.1, bf16[2,1,160,2560]{3,2,1,0:T(8,128)(2,1)} %v_ref.1), custom_call_target="tpu_custom_call" | custom-call | bytes 200000000 | tf_op jit(solution)/shard_map/spread_heads/pallas_call | solution.py:161
  119.1 0.0 copy-start
  119.1 2.5 %copy-done = bf16[6,4,160,640]{3,2,1,0:T(8,128)(2,1)S(1)} copy-done((bf16[6,4,160,640]{3,2,1,0:T(8,128)(2,1)S(1)}, bf16[6,4,160,640]{3,2,1,0:T(8,128)(2,1)}, u32[]{:S(2)}) %copy-start) | copy-done | bytes 4915224
  121.6 0.0 copy-start.1
  121.6 2.4 %copy-done.1 = bf16[6,4,160,640]{3,2,1,0:T(8,128)(2,1)S(1)} copy-done((bf16[6,4,160,640]{3,2,1,0:T(8,128)(2,1)S(1)}, bf16[6,4,160,640]{3,2,1,0:T(8,128)(2,1)}, u32[]{:S(2)}) %copy-start.1) | copy-done | bytes 4915224
  124.0 0.0 copy-start.3
  124.0 1.4 copy-done.3
  125.5 0.0 copy-start.4
  125.5 30.8 %attend.1.o_ref = bf16[4,2,160,640]{3,2,1,0:T(8,128)(2,1)S(1)} custom-call(s32[60]{0:T(128)S(1)} %reshape.20.radius_ref, bf16[4,2,160,640]{3,2,1,0:T(8,128)(2,1)S(1)} %copy-done.3, bf16[6,4,160,640]{3,2,1,0:T(8,128)(2,1)S(1)} %copy-done, bf16[6,4,160,640]{3,2,1,0:T(8,128)(2,1)S(1)} %copy-done.1), custom_call_target="tpu_custom_call" | custom-call | flops 3000000000 | bytes 14000000 | tf_op jit(solution)/shard_map/attend/pallas_call | solution.py:234
  156.3 0.0 copy-start.2
  156.3 1.2 copy-done.2
  157.4 0.0 all-gather.2.cloned.1.call-done.w_hbm
  157.4 0.0 copy-done.4
  157.4 61.4 %project_and_reduce.1 = (bf16[2,160,2560]{2,1,0:T(8,128)(2,1)S(1)}, bf16[2,160,2560]{2,1,0:T(8,128)(2,1)S(1)}, f32[2,64,2560]{2,1,0:T(8,128)S(1)}) custom-call(bf16[4,2,160,640]{3,2,1,0:T(8,128)(2,1)} %copy-done.2, bf16[2560,2560]{1,0:T(8,128)(2,1)} %all-gather.2.cloned.1.call-done.w_hbm, bf16[2,160,2560]{2,1,0:T(8,128)(2,1)} %bitcast.15, ...), custom_call_target="tpu_custom_call" | custom-call | flops 8999999488 | bytes 100000000 | tf_op jit(solution)/shard_map/project_and_reduce/pallas_call | solution.py:448
  218.9 1.1 slice_bitcast_fusion
  220.0 1.2 copy.22
  221.2 1.2 copy.23
Async XLA Ops:
  7.2 150.3 %all-gather.2.cloned.1.call-start = ((), (), s32[]{:S(2)}) async-start(), calls=%async_computation | async-start | bytes 13926400 | tf_op jit(solution)/shard_map/all_gather | solution.py:481
  119.1 2.5 %copy-start = (bf16[6,4,160,640]{3,2,1,0:T(8,128)(2,1)S(1)}, bf16[6,4,160,640]{3,2,1,0:T(8,128)(2,1)}, u32[]{:S(2)}) copy-start(bf16[6,4,160,640]{3,2,1,0:T(8,128)(2,1)} %get-tuple-element.11.k_ref) | copy-start | bytes 14745604
  121.6 2.4 %copy-start.1 = (bf16[6,4,160,640]{3,2,1,0:T(8,128)(2,1)S(1)}, bf16[6,4,160,640]{3,2,1,0:T(8,128)(2,1)}, u32[]{:S(2)}) copy-start(bf16[6,4,160,640]{3,2,1,0:T(8,128)(2,1)} %get-tuple-element.12.v_ref) | copy-start | bytes 14745604
  124.0 1.4 copy-start.3
  125.5 32.0 %copy-start.4 = (bf16[64,2560]{1,0:T(8,128)(2,1)S(1)}, bf16[64,2560]{1,0:T(8,128)(2,1)}, u32[]{:S(2)}) copy-start(bf16[64,2560]{1,0:T(8,128)(2,1)} %up_ref.1) | copy-start | bytes 983044
  156.3 1.2 copy-start.2
Sparse Core Ops, SparseCore 0:
  9.7 123.9 all-gather.1

commit v2 on v1

v2 whole, which is shorter than its diff:
```python
import functools
import math

import jax
import jax.numpy as jnp
from jax import lax
from jax.experimental import pallas as pl
from jax.experimental.pallas import tpu as pltpu
from jax.sharding import PartitionSpec as P

HEADS = 20
HEAD_DIM = 128
TILE_W = 16
COLS = 160
HALF = COLS // 2
WINDOW = 128
RANK = 64
ADAPTER_SCALE = 2.0
GRID = 16
CHIPS = 4
GROUP_HEADS = HEADS // CHIPS
GROUP = GROUP_HEADS * HEAD_DIM
WIDTH = HEADS * HEAD_DIM
NEG = -1e30
MESH = pl.DeviceIdType.MESH
BF = jnp.bfloat16
F32 = jnp.float32


def place():
    tm, height = lax.axis_index("tm"), lax.axis_index("height")
    z, xh = tm // 2, tm % 2
    y, xl, core = height // 4, (height // 2) % 2, height % 2
    return z, xh, y, xl, core


def device(z, x, y, core):
    return (z * 2 + x // 2, y * 4 + (x % 2) * 2 + core)


def enter(partners):
    barrier = pltpu.get_barrier_semaphore()
    for partner in partners:
        pl.semaphore_signal(barrier, inc=1, device_id=partner, device_id_type=MESH)
    pl.semaphore_wait(barrier, len(partners))


def remote(src, dst, send, recv, target):
    return pltpu.make_async_remote_copy(
        src_ref=src, dst_ref=dst, send_sem=send, recv_sem=recv, device_id=target, device_id_type=MESH
    )


def arrived(dst, sem):
    pltpu.make_async_copy(dst, dst, sem).wait()


def group_columns(x):
    return pl.ds(pl.multiple_of(x * GROUP, 128), GROUP)


def attend(j, f, half, radii, frame, row_first, q_ref, k_ref, v_ref, o_ref):
    radius_frame, radius_row, radius_column = radii
    start = (COLS - WINDOW) * half
    query_tile = (lax.broadcasted_iota(jnp.int32, (HALF, WINDOW), 0) + half * HALF) // TILE_W
    key_tile = (lax.broadcasted_iota(jnp.int32, (HALF, WINDOW), 1) + start) // TILE_W
    near = jnp.abs(query_tile - key_tile) <= radius_column
    query_rows, key_rows = pl.ds(half * HALF, HALF), pl.ds(start, WINDOW)
    places = [(a, b) for a in range(3) for b in range(4)]
    q = jnp.concatenate([q_ref[j, f, r, query_rows, :] for r in range(2)], axis=0)
    k = jnp.concatenate([k_ref[j, f + a, b, key_rows, :] for a, b in places], axis=0)
    v = jnp.concatenate([v_ref[j, f + a, b, key_rows, :] for a, b in places], axis=0)
    scores = lax.dot_general(q, k, (((1,), (1,)), ((), ())), preferred_element_type=F32)
    scale = math.log2(math.e) / math.sqrt(HEAD_DIM)
    nothing = jnp.zeros((HALF, WINDOW), BF)
    rows = []
    for r in range(2):
        masked = {}
        for at, (a, b) in enumerate(places):
            if not r <= b <= r + 2:
                continue
            s = scores[r * HALF : (r + 1) * HALF, at * WINDOW : (at + 1) * WINDOW]
            allowed = near
            if a != 1 or b != r + 1:
                other_frame, other_row = frame + (a - 1), row_first + (b - 1)
                inside = (
                    (other_frame >= 0) & (other_frame < GRID) & (other_row >= 0) & (other_row < GRID)
                )
                if a != 1:
                    inside = inside & (radius_frame > 0)
                if b != r + 1:
                    inside = inside & (radius_row > 0)
                allowed = near & inside
            masked[a, b] = jnp.where(allowed, s, NEG)
        highest = jnp.max(functools.reduce(jnp.maximum, masked.values()), axis=1, keepdims=True)
        weights = {at: jnp.exp2((s - highest) * scale) for at, s in masked.items()}
        total = jnp.sum(functools.reduce(jnp.add, weights.values()), axis=1, keepdims=True)
        share = 1.0 / total
        rows.append(
            jnp.concatenate(
                [(weights[at] * share).astype(BF) if at in weights else nothing for at in places], axis=1
            )
        )
    result = jnp.dot(jnp.concatenate(rows, axis=0), v, preferred_element_type=F32).astype(BF)
    for r in range(2):
        o_ref[j, f, r, query_rows, :] = result[r * HALF : (r + 1) * HALF]


def step_kernel(
    factor, radius_ref, q_hbm, k_hbm, v_hbm, w_hbm, g_hbm, down_ref, up_ref,
    mixed_ref, back_ref, grads_ref,
    qs_ref, ks_ref, vs_ref, os_ref, w_ref, g_ref, att_ref,
    part_ref, ra_ref, acc_ref, rb_ref, sum_ref, rc_ref, rd_ref, fin_ref,
    load_sem, out_sem, in_sem, halo_out, halo_in, o_out, o_in,
    wx_sem, wy_out, wy_in, wz_out, wz_in, wf_out, wf_in, ws_out, ws_in,
    a_out, a_in, b_out, b_in, c_out, c_in, d_out, d_in, e_out, e_in,
):
    z, xh, y, xl, core = place()
    x = xh * 2 + xl
    here = xl == core
    ring = x * 2 + core
    band = y * 2 + core
    before, after = (band + 7) % 8, (band + 1) % 8
    left = device(z, x, before // 2, before % 2)
    right = device(z, x, after // 2, after % 2)
    sibling = device(z, x, y, 1 - core)

    def ring_device(step):
        other = (ring + step) % 8
        return other // 2, other % 2, device(z, other // 2, y, other % 2)

    def y_device(step):
        return device(z, x, (y + step) % 4, core)

    def z_device(step):
        return device((z + step) % 4, x, y, core)

    up, down = z_device(3), z_device(1)

    def head_columns(chip, j):
        return pl.ds(pl.multiple_of((chip * GROUP_HEADS + j) * HEAD_DIM, HEAD_DIM), HEAD_DIM)

    own_weight = w_ref.at[y * 2 + xl, core, :, group_columns(z)]
    load_gradient = pltpu.make_async_copy(g_hbm, g_ref, load_sem.at[0])
    load_weight = pltpu.make_async_copy(w_hbm.at[:, group_columns(z)], own_weight, load_sem.at[1])
    load_gradient.start()
    load_weight.start()

    outside = (band + 7 + 2 * core) % 8
    enter(
        [ring_device(step)[2] for step in range(1, 8)]
        + [y_device(step) for step in range(1, 4)]
        + [z_device(step) for step in range(1, 4)]
        + [device(z, x, outside // 2, outside % 2)]
    )

    arrays = ((k_hbm, ks_ref, 1), (v_hbm, vs_ref, 1), (q_hbm, qs_ref, 0))

    def exchange(i, j, step):
        src, dst, pad = arrays[i]
        target = (x + step) % CHIPS
        piece = src.at[:, 0, :, head_columns(target, j)]
        slot = dst.at[j, pl.ds(pad + 2 * xh, 2), pad + core]
        return piece, slot, remote(
            piece, slot, out_sem.at[i, j, step], in_sem.at[i, j, xh * 2 + core],
            device(z, target, y, xl),
        )

    def give(i, j):
        for step in (2, 1, 3):
            exchange(i, j, step)[2].start()
        piece, slot, copy = exchange(i, j, 0)

        @pl.when(here)
        def _():
            pltpu.make_async_copy(piece, slot, in_sem.at[i, j, xh * 2 + core]).start()

        @pl.when(jnp.logical_not(here))
        def _():
            copy.start()

    def landed(i, j):
        _, dst, pad = arrays[i]
        for source in range(4):
            arrived(
                dst.at[j, pl.ds(pad + 2 * (source // 2), 2), pad + source % 2], in_sem.at[i, j, source]
            )

    def halos(i, j):
        ref = arrays[i][1].at[j]

        def send(n, src, dst, target):
            return remote(src, dst, halo_out.at[i, j, n], halo_in.at[i, j, n], target)

        rows, own = pl.ds(1, 2), pl.ds(1, 4)
        return (
            send(0, ref.at[1, rows], ref.at[5, rows], up),
            send(1, ref.at[4, rows], ref.at[0, rows], down),
            send(2, ref.at[own, 1], ref.at[own, 3], left),
            send(3, ref.at[own, 2], ref.at[own, 0], right),
            send(4, ref.at[0, 1], ref.at[0, 3], left),
            send(5, ref.at[5, 1], ref.at[5, 3], left),
            send(6, ref.at[0, 2], ref.at[0, 0], right),
            send(7, ref.at[5, 2], ref.at[5, 0], right),
        )

    def start_halos(j):
        for i in range(2):
            landed(i, j)
            for copy in halos(i, j)[:4]:
                copy.start()

    def start_corners(j):
        for i in range(2):
            copies = halos(i, j)
            copies[0].wait_recv()
            copies[1].wait_recv()
            for copy in copies[4:]:
                copy.start()

    def await_head(j):
        for i in range(2):
            for copy in halos(i, j)[2:]:
                copy.wait_recv()
        landed(2, j)

    def attend_frames(j, first, last):
        head = x * GROUP_HEADS + j
        radii = [radius_ref[head, n] for n in range(3)]

        def one(f, carry):
            for half in range(2):
                attend(
                    j, f, half, radii, z * 4 + f, y * 4 + core * 2, qs_ref, ks_ref, vs_ref, os_ref
                )
            return carry

        lax.fori_loop(first, last, one, 0)

    def give_back(j, n):
        frames = (xh + n // 2) % 2
        row = (core + n % 2) % 2
        piece = os_ref.at[j, pl.ds(2 * frames, 2), row]
        slot = att_ref.at[:, :, head_columns(x, j)]
        return piece, slot, remote(
            piece, slot, o_out.at[j, n], o_in.at[j, x], device(z, frames * 2 + core, y, row)
        )

    def start_back(j):
        for n in (2, 3, 1):
            give_back(j, n)[2].start()
        piece, slot, copy = give_back(j, 0)

        @pl.when(here)
        def _():
            pltpu.make_async_copy(piece, slot, o_in.at[j, x]).start()

        @pl.when(jnp.logical_not(here))
        def _():
            copy.start()

    def weight_piece(quarter, n, side):
        return w_ref.at[pl.ds(2 * ((y + n) % 4), 2), side, :, group_columns((z + quarter) % 4)]

    weight_x = remote(
        own_weight, own_weight, wx_sem.at[0], wx_sem.at[1], device(z, xh * 2 + 1 - xl, y, core)
    )

    def weight_y(step):
        piece = weight_piece(0, 0, core)
        return remote(piece, piece, wy_out.at[step - 1], wy_in.at[3 - step], y_device(step))

    def weight_z(way, n):
        piece = weight_piece(0, n, core)
        return remote(piece, piece, wz_out.at[way, n], wz_in.at[way, n], (up, down)[way])

    def weight_forward(n):
        piece = weight_piece(3 if n < 2 else 1, n, core)
        return remote(piece, piece, wf_out.at[n], wf_in.at[n], down if n < 2 else up)

    def weight_sibling(quarter, n):
        piece = weight_piece(quarter, n, core)
        return remote(piece, piece, ws_out.at[quarter, n], ws_in.at[quarter, n], sibling)

    def spread_weight(n):
        weight_z(0, n).start()
        weight_z(1, n).start()
        weight_sibling(0, n).start()

    def take_weight_y(n):
        arrived(weight_piece(0, n, core), wy_in.at[n - 1])

    def pass_weight(n):
        arrived(weight_piece(1, n, core), wz_in.at[0, n])
        arrived(weight_piece(3, n, core), wz_in.at[1, n])
        weight_forward(n).start()
        weight_sibling(1, n).start()
        weight_sibling(3, n).start()

    def last_weight(n):
        arrived(weight_piece(2, n, core), wf_in.at[n])
        weight_sibling(2, n).start()

    K, V, Q = 0, 1, 2
    for i, j in ((K, 0), (V, 0), (K, 1), (V, 1), (Q, 0)):
        give(i, j)
    load_weight.wait()
    weight_x.start()
    load_gradient.wait()
    contract_last = (((1,), (1,)), ((), ()))
    contract_first = (((0,), (0,)), ((), ()))
    tokens = 2 * COLS
    low_back = lax.dot_general(
        g_ref[...].reshape(tokens, WIDTH), up_ref[...], contract_last, preferred_element_type=F32
    ).astype(BF)

    start_halos(0)
    for i, j in ((K, 2), (V, 2), (Q, 1)):
        give(i, j)
    weight_x.wait_recv()
    for step in (2, 1, 3):
        weight_y(step).start()
    spread_weight(0)
    start_corners(0)

    start_halos(1)
    for i, j in ((K, 3), (V, 3), (Q, 2)):
        give(i, j)
    await_head(0)
    attend_frames(0, 0, 4)
    start_back(0)
    start_corners(1)
    take_weight_y(1)
    spread_weight(1)
    take_weight_y(3)
    spread_weight(3)

    start_halos(2)
    for i, j in ((K, 4), (V, 4), (Q, 3), (Q, 4)):
        give(i, j)
    await_head(1)
    attend_frames(1, 0, 4)
    start_back(1)
    start_corners(2)
    take_weight_y(2)
    spread_weight(2)
    pass_weight(0)

    start_halos(3)
    await_head(2)
    attend_frames(2, 0, 4)
    start_back(2)
    start_corners(3)
    pass_weight(1)

    start_halos(4)
    await_head(3)
    attend_frames(3, 0, 2)
    start_corners(4)
    attend_frames(3, 2, 4)
    start_back(3)
    await_head(4)
    attend_frames(4, 0, 4)
    start_back(4)
    pass_weight(3)
    pass_weight(2)

    for j in range(GROUP_HEADS):
        for source in range(CHIPS):
            arrived(att_ref.at[:, :, head_columns(source, j)], o_in.at[j, source])
    low = jnp.dot(
        att_ref[...].reshape(tokens, WIDTH), down_ref[...], preferred_element_type=F32
    ).astype(BF)
    part_ref[0] = (
        factor
        * lax.dot_general(
            low, g_ref[...].reshape(tokens, WIDTH), contract_first, preferred_element_type=F32
        )
    ).astype(BF)
    part_ref[1] = (
        factor
        * lax.dot_general(
            low_back, att_ref[...].reshape(tokens, WIDTH), contract_first, preferred_element_type=F32
        )
    ).astype(BF)

    def phase_a(step):
        tx, tc, target = ring_device(step)
        return remote(
            part_ref.at[tc, :, group_columns(tx)], ra_ref.at[step - 1],
            a_out.at[step - 1], a_in.at[step - 1], target,
        )

    for step in range(1, 8):
        phase_a(step).start()

    step_width = 256

    def forward(j, carry):
        columns = pl.ds(pl.multiple_of(j * step_width, step_width), step_width)
        frozen = jnp.dot(
            att_ref[...].reshape(tokens, WIDTH), w_ref[:, :, :, columns].reshape(WIDTH, step_width),
            preferred_element_type=F32,
        )
        adapter = jnp.dot(low, up_ref[:, columns], preferred_element_type=F32)
        mixed_ref[:, :, columns] = (
            (frozen + ADAPTER_SCALE * adapter).astype(BF).reshape(2, COLS, step_width)
        )
        return carry

    def backward(j, carry):
        rows = group_columns(j)
        frozen = lax.dot_general(
            g_ref[...].reshape(tokens, WIDTH), w_ref[pl.ds(2 * j, 2)].reshape(GROUP, WIDTH),
            contract_last, preferred_element_type=F32,
        )
        adapter = lax.dot_general(
            low_back, down_ref[rows, :], contract_last, preferred_element_type=F32
        )
        back_ref[:, :, rows] = (
            (frozen + ADAPTER_SCALE * adapter).astype(BF).reshape(2, COLS, GROUP)
        )
        return carry

    def from_sibling(quarter):
        for n in range(4):
            arrived(weight_piece(quarter, n, 1 - core), ws_in.at[quarter, n])

    half_blocks = WIDTH // step_width // 2
    near_half = z // 2
    near_quarter = 1 + 2 * (z % 2)
    from_sibling(0)
    from_sibling(near_quarter)
    lax.fori_loop(near_half * half_blocks, (near_half + 1) * half_blocks, forward, 0)
    for n in (0, 1, 3, 2):
        last_weight(n)

    total = part_ref[core, :, group_columns(x)].astype(F32)
    for step in range(1, 8):
        phase_a(step).wait_recv()
        total = total + ra_ref[step - 1].astype(F32)
    acc_ref[...] = total

    def chunk(n):
        return pl.ds(pl.multiple_of(n * 16, 16), 16)

    def phase_b(step):
        return remote(
            acc_ref.at[chunk((y + step) % 4)], rb_ref.at[step - 1],
            b_out.at[step - 1], b_in.at[step - 1], y_device(step),
        )

    for step in range(1, 4):
        phase_b(step).start()
    total = acc_ref[chunk(y), :]
    for step in range(1, 4):
        phase_b(step).wait_recv()
        total = total + rb_ref[step - 1]
    sum_ref[...] = total

    def phase_c(step):
        return remote(
            sum_ref, rc_ref.at[step - 1], c_out.at[step - 1], c_in.at[step - 1], z_device(step)
        )

    for step in range(1, 4):
        phase_c(step).start()
    for step in range(1, 4):
        phase_c(step).wait_recv()

    total = jnp.zeros((16, GROUP), F32)
    for source in range(4):
        back = (z - source + 4) % 4
        term = sum_ref[...]
        for step in range(1, 4):
            term = jnp.where(back == step, rc_ref[step - 1], term)
        total = total + term
    rd_ref[chunk(y), :] = total.astype(BF)

    def phase_d(step):
        return remote(
            rd_ref.at[chunk(y)], rd_ref.at[chunk(y)],
            d_out.at[step - 1], d_in.at[step - 1], y_device(step),
        )

    for step in range(1, 4):
        phase_d(step).start()
    for step in range(1, 4):
        arrived(rd_ref.at[chunk((y - step + 4) % 4)], d_in.at[step - 1])

    def phase_e(step):
        return remote(
            rd_ref, fin_ref.at[core, :, group_columns(x)],
            e_out.at[step - 1], e_in.at[step - 1], ring_device(step)[2],
        )

    for step in range(1, 8):
        phase_e(step).start()
    fin_ref[core, :, group_columns(x)] = rd_ref[...]

    from_sibling(4 - near_quarter)
    from_sibling(2)
    lax.fori_loop((1 - near_half) * half_blocks, (2 - near_half) * half_blocks, forward, 0)
    lax.fori_loop(0, CHIPS, backward, 0)

    for step in range(1, 8):
        other = (ring - step + 8) % 8
        arrived(fin_ref.at[other % 2, :, group_columns(other // 2)], e_in.at[step - 1])
    grads_ref[...] = fin_ref[...].astype(F32)

    for j in range(GROUP_HEADS):
        for i in range(3):
            for step in (2, 1, 3):
                exchange(i, j, step)[2].wait_send()
        for i in range(2):
            for copy in halos(i, j):
                copy.wait_send()
        for n in (2, 3, 1):
            give_back(j, n)[2].wait_send()

    @pl.when(jnp.logical_not(here))
    def _():
        for j in range(GROUP_HEADS):
            for i in range(3):
                exchange(i, j, 0)[2].wait_send()
            give_back(j, 0)[2].wait_send()

    weight_x.wait_send()
    for step in range(1, 4):
        weight_y(step).wait_send()
    for n in range(4):
        weight_z(0, n).wait_send()
        weight_z(1, n).wait_send()
        weight_forward(n).wait_send()
        for quarter in range(4):
            weight_sibling(quarter, n).wait_send()
    for step in range(1, 8):
        phase_a(step).wait_send()
        phase_e(step).wait_send()
    for step in range(1, 4):
        phase_b(step).wait_send()
        phase_c(step).wait_send()
        phase_d(step).wait_send()


def per_device(
    queries, keys, values, head_window_radius, output_weight, adapter_down_weight, adapter_up_weight,
    output_gradient,
):
    factor = ADAPTER_SCALE / math.sqrt(GRID * GRID * COLS)
    vmem = pl.BlockSpec(memory_space=pltpu.VMEM)
    smem = pl.BlockSpec(memory_space=pltpu.SMEM)
    hbm = pl.BlockSpec(memory_space=pl.ANY)
    block = jax.ShapeDtypeStruct((2, COLS, WIDTH), BF)
    dma = pltpu.SemaphoreType.DMA
    mixed, back, grads = pl.pallas_call(
        functools.partial(step_kernel, factor),
        out_shape=(block, block, jax.ShapeDtypeStruct((2, RANK, WIDTH), F32)),
        in_specs=[smem, hbm, hbm, hbm, hbm, hbm, vmem, vmem],
        out_specs=(vmem,) * 3,
        scratch_shapes=[
            pltpu.VMEM((GROUP_HEADS, 4, 2, COLS, HEAD_DIM), BF),
            pltpu.VMEM((GROUP_HEADS, 6, 4, COLS, HEAD_DIM), BF),
            pltpu.VMEM((GROUP_HEADS, 6, 4, COLS, HEAD_DIM), BF),
            pltpu.VMEM((GROUP_HEADS, 4, 2, COLS, HEAD_DIM), BF),
            pltpu.VMEM((8, 2, COLS, WIDTH), BF),
            pltpu.VMEM((2, COLS, WIDTH), BF),
            pltpu.VMEM((2, COLS, WIDTH), BF),
            pltpu.VMEM((2, RANK, WIDTH), BF),
            pltpu.VMEM((7, RANK, GROUP), BF),
            pltpu.VMEM((RANK, GROUP), F32),
            pltpu.VMEM((3, 16, GROUP), F32),
            pltpu.VMEM((16, GROUP), F32),
            pltpu.VMEM((3, 16, GROUP), F32),
            pltpu.VMEM((RANK, GROUP), BF),
            pltpu.VMEM((2, RANK, WIDTH), BF),
            dma((2,)), dma((3, GROUP_HEADS, 4)), dma((3, GROUP_HEADS, 4)),
            dma((2, GROUP_HEADS, 8)), dma((2, GROUP_HEADS, 8)),
            dma((GROUP_HEADS, 4)), dma((GROUP_HEADS, 4)),
            dma((2,)), dma((3,)), dma((3,)), dma((2, 4)), dma((2, 4)), dma((4,)), dma((4,)),
            dma((4, 4)), dma((4, 4)),
            dma((7,)), dma((7,)), dma((3,)), dma((3,)),
            dma((3,)), dma((3,)), dma((3,)), dma((3,)), dma((7,)), dma((7,)),
        ],
        compiler_params=pltpu.CompilerParams(
            collective_id=0, has_side_effects=True, vmem_limit_bytes=56 * 2**20
        ),
        cost_estimate=pl.CostEstimate(
            flops=14_000_000_000, bytes_accessed=100_000_000, transcendentals=7_000_000
        ),
        name="training_step",
    )(
        head_window_radius, queries, keys, values, output_weight,
        output_gradient.reshape(2, COLS, WIDTH), adapter_down_weight, adapter_up_weight,
    )
    shape = (2, 1, COLS, WIDTH)
    return mixed.reshape(shape), back.reshape(shape), grads[0], grads[1].T


def solution(mesh):
    tokens = P("tm", "height", None, None)
    return jax.shard_map(
        per_device,
        mesh=mesh,
        in_specs=(tokens, tokens, tokens, P(), P("height", None), P(), P(), tokens),
        out_specs=(tokens, tokens, P(), P()),
        check_vma=False,
    )
```

time: 230 us -> 183 us (0.80)
  Pallas kernels: 201 us -> 173 us
  between operations: 14.1 us -> 0.65 us
  local copies, waits for them, and re-layouts: 13.2 us -> 9.16 us
    pallas_call x3 -> x1, Pallas kernels: 201 us -> 173 us  [per_device(): pl.pallas_call(functools.partial(step_kernel, factor), out_shape=(block,...]
    unnamed x14 -> x8, local copies, waits for them, and re-layouts: 11.9 us -> 6.61 us
  transfers between devices with their start and end apart: 1 -> 0, of which waited for: 0 -> 0; matrix products, arithmetic and copies ran while one was open for 1% -> 0% of each run, Pallas kernels for 61% -> 0%
where the time goes in v2:
time: 183 us
  Pallas kernels  173 us (95%)
  local copies, waits for them, and re-layouts  9.16 us (5%)
    pallas_call x1, Pallas kernels, per_device(): pl.pallas_call(functools.partial(step_kernel, factor), out_shape=(block,...  173 us
    unnamed x8, local copies, waits for them, and re-layouts  6.61 us

profile of v2, /device:TPU:1, one launch (start us, length us, event | category | flops | bytes accessed | tf_op | source)
XLA Modules:
  0.0 183.0 jit_solution(10222586272107580677)
XLA Ops:
  0.6 1.4 copy.12.radius_ref
  2.0 2.1 %copy.13.down_ref = bf16[2560,64]{1,0:T(8,128)(2,1)} copy(bf16[2560,64]{0,1:T(8,128)(2,1)} %param.13) | data formatting | bytes 655360 | tf_op args[5]
  4.0 173.2 %training_step.1 = (bf16[2,160,2560]{2,1,0:T(8,128)(2,1)}, bf16[2,160,2560]{2,1,0:T(8,128)(2,1)}, f32[2,64,2560]{2,1,0:T(8,128)}) custom-call(s32[20,3]{1,0:T(8,128)} %copy.12.radius_ref, bf16[2,1,160,2560]{3,2,1,0:T(8,128)(2,1)} %q_hbm.1, bf16[2,1,160,2560]{3,2,1,0:T(8,128)(2,1)} %k_hbm.1, bf16[2,1,160,2560]{3,2,1,0:T(8,128)(2,1)} %v_hbm.1, ...), custom_call_target="tpu_custom_call" | custom-call | flops 14000000000 | bytes 100000000 | tf_op jit(solution)/shard_map/training_step/pallas_call | solution.py:556
  177.3 0.0 copy-start.1
  177.3 2.6 %slice_bitcast_fusion = (f32[2560,64]{0,1:T(8,128)}, f32[64,2560]{1,0:T(8,128)}) fusion(f32[2,64,2560]{2,1,0:T(8,128)} %get-tuple-element.9), kind=kLoop, calls=%fused_computation | loop fusion | bytes 2621440 | tf_op jit(solution)/shard_map/transpose | solution.py:597
  179.9 0.0 copy-done.1
  179.9 0.0 copy-start
  179.9 1.2 copy.18
  181.0 0.9 copy-done
  181.9 1.2 copy.19
Async XLA Ops:
  177.3 2.6 %copy-start.1 = (bf16[2,160,2560]{2,1,0:T(8,128)(2,1)S(1)}, bf16[2,160,2560]{2,1,0:T(8,128)(2,1)}, u32[]{:S(2)}) copy-start(bf16[2,160,2560]{2,1,0:T(8,128)(2,1)} %get-tuple-element.7) | copy-start | bytes 4915204
  179.9 2.0 %copy-start = (bf16[2,160,2560]{2,1,0:T(8,128)(2,1)S(1)}, bf16[2,160,2560]{2,1,0:T(8,128)(2,1)}, u32[]{:S(2)}) copy-start(bf16[2,160,2560]{2,1,0:T(8,128)(2,1)} %get-tuple-element.8) | copy-start | bytes 4915204

commit v3 on v2

v3 whole, which is shorter than its diff:
```python
import functools
import math

import jax
import jax.numpy as jnp
from jax import lax
from jax.experimental import pallas as pl
from jax.experimental.pallas import tpu as pltpu
from jax.sharding import PartitionSpec as P

HEADS = 20
HEAD_DIM = 128
TILE_W = 16
COLS = 160
HALF = COLS // 2
WINDOW = 128
RANK = 64
ADAPTER_SCALE = 2.0
GRID = 16
CHIPS = 4
GROUP_HEADS = HEADS // CHIPS
GROUP = GROUP_HEADS * HEAD_DIM
WIDTH = HEADS * HEAD_DIM
NEG = -1e30
MESH = pl.DeviceIdType.MESH
BF = jnp.bfloat16
F32 = jnp.float32


def place():
    tm, height = lax.axis_index("tm"), lax.axis_index("height")
    z, xh = tm // 2, tm % 2
    y, xl, core = height // 4, (height // 2) % 2, height % 2
    return z, xh, y, xl, core


def device(z, x, y, core):
    return (z * 2 + x // 2, y * 4 + (x % 2) * 2 + core)


def enter(partners):
    barrier = pltpu.get_barrier_semaphore()
    for partner in partners:
        pl.semaphore_signal(barrier, inc=1, device_id=partner, device_id_type=MESH)
    pl.semaphore_wait(barrier, len(partners))


def remote(src, dst, send, recv, target):
    return pltpu.make_async_remote_copy(
        src_ref=src, dst_ref=dst, send_sem=send, recv_sem=recv, device_id=target, device_id_type=MESH
    )


def arrived(dst, sem):
    pltpu.make_async_copy(dst, dst, sem).wait()


def group_columns(x):
    return pl.ds(pl.multiple_of(x * GROUP, 128), GROUP)


def attend(j, f, half, radii, frame, row_first, q_ref, k_ref, v_ref, o_ref):
    radius_frame, radius_row, radius_column = radii
    start = (COLS - WINDOW) * half
    query_tile = (lax.broadcasted_iota(jnp.int32, (HALF, WINDOW), 0) + half * HALF) // TILE_W
    key_tile = (lax.broadcasted_iota(jnp.int32, (HALF, WINDOW), 1) + start) // TILE_W
    near = jnp.abs(query_tile - key_tile) <= radius_column
    query_rows, key_rows = pl.ds(half * HALF, HALF), pl.ds(start, WINDOW)
    places = [(a, b) for a in range(3) for b in range(4)]
    q = jnp.concatenate([q_ref[j, f, r, query_rows, :] for r in range(2)], axis=0)
    k = jnp.concatenate([k_ref[j, f + a, b, key_rows, :] for a, b in places], axis=0)
    v = jnp.concatenate([v_ref[j, f + a, b, key_rows, :] for a, b in places], axis=0)
    scores = lax.dot_general(q, k, (((1,), (1,)), ((), ())), preferred_element_type=F32)
    scale = math.log2(math.e) / math.sqrt(HEAD_DIM)
    nothing = jnp.zeros((HALF, WINDOW), BF)
    rows = []
    for r in range(2):
        masked = {}
        for at, (a, b) in enumerate(places):
            if not r <= b <= r + 2:
                continue
            s = scores[r * HALF : (r + 1) * HALF, at * WINDOW : (at + 1) * WINDOW]
            allowed = near
            if a != 1 or b != r + 1:
                other_frame, other_row = frame + (a - 1), row_first + (b - 1)
                inside = (
                    (other_frame >= 0) & (other_frame < GRID) & (other_row >= 0) & (other_row < GRID)
                )
                if a != 1:
                    inside = inside & (radius_frame > 0)
                if b != r + 1:
                    inside = inside & (radius_row > 0)
                allowed = near & inside
            masked[a, b] = jnp.where(allowed, s, NEG)
        highest = jnp.max(functools.reduce(jnp.maximum, masked.values()), axis=1, keepdims=True)
        weights = {at: jnp.exp2((s - highest) * scale) for at, s in masked.items()}
        total = jnp.sum(functools.reduce(jnp.add, weights.values()), axis=1, keepdims=True)
        share = 1.0 / total
        rows.append(
            jnp.concatenate(
                [(weights[at] * share).astype(BF) if at in weights else nothing for at in places], axis=1
            )
        )
    result = jnp.dot(jnp.concatenate(rows, axis=0), v, preferred_element_type=F32).astype(BF)
    for r in range(2):
        o_ref[j, f, r, query_rows, :] = result[r * HALF : (r + 1) * HALF]


def step_kernel(
    factor, radius_ref, q_hbm, k_hbm, v_hbm, w_hbm, g_hbm, down_hbm, up_hbm,
    mixed_hbm, back_hbm, grads_hbm,
    mixed_ref, back_ref,
    qs_ref, ks_ref, vs_ref, os_ref, w_ref, g_ref, att_ref,
    part_ref, ra_ref, acc_ref, rb_ref, rd_ref, fin_ref,
    down_ref, up_ref, own_back_ref, back_low_ref, back_turned_ref, down_part_ref, down_got_ref,
    load_sem, out_sem, in_sem, halo_out, halo_in, o_in, p_sem,
    w_out, wx_in, wy_in, wz_in, ws_in, r_sem, e_in, store_sem,
):
    z, xh, y, xl, core = place()
    x = xh * 2 + xl
    here = xl == core
    ring = x * 2 + core
    band = y * 2 + core
    before, after = (band + 7) % 8, (band + 1) % 8
    left = device(z, x, before // 2, before % 2)
    right = device(z, x, after // 2, after % 2)
    sibling = device(z, x, y, 1 - core)

    def ring_device(step):
        other = (ring + step) % 8
        return other // 2, other % 2, device(z, other // 2, y, other % 2)

    def y_device(step):
        return device(z, x, (y + step) % 4, core)

    def z_device(step):
        return device((z + step) % 4, x, y, core)

    up, down = z_device(3), z_device(1)

    def head_columns(chip, j):
        return pl.ds(pl.multiple_of((chip * GROUP_HEADS + j) * HEAD_DIM, HEAD_DIM), HEAD_DIM)

    load_gradient = pltpu.make_async_copy(g_hbm, g_ref, load_sem.at[0])
    load_weight = [
        pltpu.make_async_copy(
            w_hbm.at[:, group_columns((z + quarter) % 4)],
            w_ref.at[y * 2 + xl, core, :, group_columns((z + quarter) % 4)],
            load_sem.at[1 + quarter // 2],
        )
        for quarter in (0, 2)
    ]
    load_up = pltpu.make_async_copy(up_hbm, up_ref, load_sem.at[3])
    load_down = pltpu.make_async_copy(down_hbm, down_ref, load_sem.at[4])
    load_gradient.start()
    load_up.start()
    load_down.start()
    for copy in load_weight:
        copy.start()

    outside = (band + 7 + 2 * core) % 8
    enter(
        [ring_device(step)[2] for step in range(1, 8)]
        + [device((z + step % 4) % 4, x, (y + step // 4) % 4, core) for step in range(1, 16)]
        + [device(z, x, outside // 2, outside % 2)]
    )

    arrays = ((k_hbm, ks_ref, 1), (v_hbm, vs_ref, 1), (q_hbm, qs_ref, 0))

    def exchange(i, j, step):
        src, dst, pad = arrays[i]
        target = (x + step) % CHIPS
        piece = src.at[:, 0, :, head_columns(target, j)]
        slot = dst.at[j, pl.ds(pad + 2 * xh, 2), pad + core]
        return piece, slot, remote(
            piece, slot, out_sem.at[0], in_sem.at[i, j],
            device(z, target, y, xl),
        )

    def give(i, j):
        for step in (2, 1, 3):
            exchange(i, j, step)[2].start()
        piece, slot, copy = exchange(i, j, 0)

        @pl.when(here)
        def _():
            pltpu.make_async_copy(piece, slot, in_sem.at[i, j]).start()

        @pl.when(jnp.logical_not(here))
        def _():
            copy.start()

    def landed(i, j):
        own = (pl.ds(1, 4), pl.ds(1, 2)) if i < 2 else ()
        arrived(arrays[i][1].at[(j, *own)], in_sem.at[i, j])

    def halos(i, j):
        ref = arrays[i][1].at[j]

        def send(n, src, dst, target):
            return remote(src, dst, halo_out.at[i], halo_in.at[i, j, min(n // 2, 1)], target)

        rows, own = pl.ds(1, 2), pl.ds(1, 4)
        return (
            send(0, ref.at[1, rows], ref.at[5, rows], up),
            send(1, ref.at[4, rows], ref.at[0, rows], down),
            send(2, ref.at[own, 1], ref.at[own, 3], left),
            send(3, ref.at[own, 2], ref.at[own, 0], right),
            send(4, ref.at[0, 1], ref.at[0, 3], left),
            send(5, ref.at[5, 1], ref.at[5, 3], left),
            send(6, ref.at[0, 2], ref.at[0, 0], right),
            send(7, ref.at[5, 2], ref.at[5, 0], right),
        )

    def start_halos(j):
        for i in range(2):
            landed(i, j)
            for copy in halos(i, j)[:4]:
                copy.start()

    def start_corners(j):
        for i in range(2):
            arrived(arrays[i][1].at[j, 0], halo_in.at[i, j, 0])
            for copy in halos(i, j)[4:]:
                copy.start()

    def await_head(j):
        for i in range(2):
            arrived(arrays[i][1].at[j, pl.ds(0, 3)], halo_in.at[i, j, 1])
        landed(2, j)

    def attend_frames(j, first, last):
        head = x * GROUP_HEADS + j
        radii = [radius_ref[n, head] for n in range(3)]

        def one(f, carry):
            for half in range(2):
                attend(
                    j, f, half, radii, z * 4 + f, y * 4 + core * 2, qs_ref, ks_ref, vs_ref, os_ref
                )
            return carry

        lax.fori_loop(first, last, one, 0)

    def give_back(j, n):
        frames = (xh + n // 2) % 2
        row = (core + n % 2) % 2
        piece = os_ref.at[j, pl.ds(2 * frames, 2), row]
        slot = att_ref.at[:, :, head_columns(x, j)]
        return piece, slot, remote(
            piece, slot, out_sem.at[1], o_in.at[0], device(z, frames * 2 + core, y, row)
        )

    def start_back(j):
        for n in (2, 3, 1):
            give_back(j, n)[2].start()
        piece, slot, copy = give_back(j, 0)

        @pl.when(here)
        def _():
            pltpu.make_async_copy(piece, slot, o_in.at[0]).start()

        @pl.when(jnp.logical_not(here))
        def _():
            copy.start()

    def weight_piece(quarter, n, side):
        return w_ref.at[pl.ds(2 * ((y + n) % 4), 2), side, :, group_columns((z + quarter) % 4)]

    def weight_shard(quarter, n, part):
        return w_ref.at[
            2 * ((y + n) % 4) + (xl + part) % 2, core, :, group_columns((z + quarter) % 4)
        ]

    def weight_x(quarter):
        piece = weight_shard(quarter, 0, 0)
        other = (xh + quarter // 2) % 2 * 2 + 1 - xl
        return remote(
            piece, piece, w_out.at[0], wx_in.at[quarter // 2],
            device(z, other, y, core),
        )

    def weight_y(quarter, step, part):
        piece = weight_shard(quarter, 0, part)
        at = quarter // 2
        return remote(
            piece, piece, w_out.at[1], wy_in.at[at, 3 - step],
            y_device(step),
        )

    def weight_z_shard(way, part):
        piece = weight_shard(0, 0, part)
        return remote(piece, piece, w_out.at[2], wz_in.at[way, 0], (up, down)[way])

    def weight_z(way, n):
        piece = weight_piece(0, n, core)
        return remote(piece, piece, w_out.at[2], wz_in.at[way, n], (up, down)[way])

    def weight_sibling(quarter, n):
        piece = weight_piece(quarter, n, core)
        return remote(piece, piece, w_out.at[3], ws_in.at[0], sibling)

    def start_y(quarter, part, steps=(1, 3, 2)):
        for step in steps:
            weight_y(quarter, step, part).start()

    def start_z_shard(part):
        for way in range(2):
            weight_z_shard(way, part).start()

    def take_y(quarter, n):
        arrived(weight_piece(quarter, n, core), wy_in.at[quarter // 2, n - 1])
        weight_sibling(quarter, n).start()

    def spread_weight(n):
        take_y(0, n)
        weight_z(0, n).start()
        weight_z(1, n).start()

    def take_z(n):
        for way, quarter in ((0, 1), (1, 3)):
            arrived(weight_piece(quarter, n, core), wz_in.at[way, n])
            weight_sibling(quarter, n).start()

    def give_low(step):
        target = (x + step) % CHIPS
        return remote(
            own_back_ref, back_low_ref.at[xh, core], out_sem.at[2], o_in.at[1],
            device(z, target, y, xl),
        )

    def add_down(j):
        total = jnp.zeros((RANK, HEAD_DIM), F32)
        for f in range(4):
            for r in range(2):
                total = total + jnp.dot(
                    back_turned_ref[f, r], os_ref[j, f, r], preferred_element_type=F32
                )
        down_part_ref[:, j * HEAD_DIM : (j + 1) * HEAD_DIM] = factor * total

    def half_rows(n):
        return pl.ds(pl.multiple_of(n * 32, 32), 32)

    down_to_sibling = remote(
        down_part_ref.at[half_rows(1 - core)], down_got_ref, p_sem.at[0], p_sem.at[1], sibling
    )

    K, V, Q = 0, 1, 2
    for copy in load_weight:
        copy.wait()
    weight_x(0).start()
    start_y(0, 0)
    start_z_shard(0)
    give(K, 0)
    give(V, 0)
    weight_x(2).start()
    load_gradient.wait()
    load_up.wait()
    load_down.wait()
    contract_last = (((1,), (1,)), ((), ()))
    contract_first = (((0,), (0,)), ((), ()))
    tokens = 2 * COLS
    low_back = lax.dot_general(
        g_ref[...].reshape(tokens, WIDTH), up_ref[...], contract_last, preferred_element_type=F32
    ).astype(BF)
    own_back_ref[...] = jnp.concatenate([low_back[:COLS], low_back[COLS:]], axis=1)
    for step in (2, 1, 3):
        give_low(step).start()
    low_copy = give_low(0)
    low_slot = back_low_ref.at[xh, core]

    @pl.when(here)
    def _():
        pltpu.make_async_copy(own_back_ref, low_slot, o_in.at[1]).start()

    @pl.when(jnp.logical_not(here))
    def _():
        low_copy.start()

    for i, j in (
        (K, 1), (V, 1), (Q, 0), (K, 2), (V, 2), (Q, 1),
        (K, 3), (V, 3), (Q, 2), (K, 4), (V, 4), (Q, 3), (Q, 4),
    ):
        give(i, j)
    weight_x(0).wait_recv()
    start_y(0, 1)
    start_z_shard(1)
    weight_sibling(0, 0).start()

    start_halos(0)
    start_corners(0)
    spread_weight(1)
    start_halos(1)
    arrived(back_low_ref, o_in.at[1])
    for pair in range(2):
        for row in range(2):
            turned = back_low_ref[pair, row].astype(F32).T.astype(BF)
            for n in range(2):
                frame = 2 * pair + n
                back_turned_ref[frame, row] = turned[n * RANK : (n + 1) * RANK]
    await_head(0)
    weight_x(2).wait_recv()
    start_y(2, 0, (1, 3))
    weight_sibling(2, 0).start()
    attend_frames(0, 0, 4)
    start_back(0)
    add_down(0)
    start_corners(1)

    start_halos(2)
    await_head(1)
    start_y(2, 0, (2,))
    spread_weight(3)
    take_z(0)
    attend_frames(1, 0, 4)
    start_back(1)
    add_down(1)
    start_corners(2)

    start_halos(3)
    await_head(2)
    start_y(2, 1, (1, 3))
    spread_weight(2)
    take_z(1)
    attend_frames(2, 0, 4)
    start_back(2)
    add_down(2)
    start_corners(3)

    start_halos(4)
    await_head(3)
    start_y(2, 1, (2,))
    take_z(3)
    attend_frames(3, 0, 2)
    start_corners(4)
    attend_frames(3, 2, 4)
    start_back(3)
    add_down(3)
    for n in range(1, 4):
        take_y(2, n)
    take_z(2)
    await_head(4)
    attend_frames(4, 0, 4)
    start_back(4)
    add_down(4)
    down_to_sibling.start()

    step_width = 256

    def forward(j, carry):
        columns = pl.ds(pl.multiple_of(j * step_width, step_width), step_width)
        frozen = jnp.dot(
            att_ref[...].reshape(tokens, WIDTH), w_ref[:, :, :, columns].reshape(WIDTH, step_width),
            preferred_element_type=F32,
        )
        adapter = jnp.dot(low, up_ref[:, columns], preferred_element_type=F32)
        mixed_ref[:, :, columns] = (
            (frozen + ADAPTER_SCALE * adapter).astype(BF).reshape(2, COLS, step_width)
        )
        return carry

    def backward(j, carry):
        rows = group_columns(j)
        frozen = lax.dot_general(
            g_ref[...].reshape(tokens, WIDTH), w_ref[pl.ds(2 * j, 2)].reshape(GROUP, WIDTH),
            contract_last, preferred_element_type=F32,
        )
        adapter = jnp.dot(low_back, down_ref[:, rows], preferred_element_type=F32)
        back_ref[:, :, rows] = (
            (frozen + ADAPTER_SCALE * adapter).astype(BF).reshape(2, COLS, GROUP)
        )
        return carry

    arrived(w_ref.at[:, 1 - core], ws_in.at[0])
    lax.fori_loop(0, CHIPS, backward, 0)
    store_back = pltpu.make_async_copy(back_ref, back_hbm, store_sem.at[0])
    store_back.start()

    arrived(att_ref, o_in.at[0])
    low = lax.dot_general(
        att_ref[...].reshape(tokens, WIDTH), down_ref[...], contract_last, preferred_element_type=F32
    ).astype(BF)
    part_ref[...] = (
        factor
        * lax.dot_general(
            low, g_ref[...].reshape(tokens, WIDTH), contract_first, preferred_element_type=F32
        )
    ).astype(BF)

    def phase_a(step):
        tx, tc, target = ring_device(step)
        return remote(
            part_ref.at[half_rows(tc), group_columns(tx)], ra_ref.at[step - 1],
            r_sem.at[0], r_sem.at[1], target,
        )

    for step in range(1, 8):
        phase_a(step).start()

    blocks = WIDTH // step_width
    lax.fori_loop(0, blocks // 2, forward, 0)
    @pl.when(here)
    def _():
        arrived(ks_ref.at[:, :, pl.ds(0, 3)], out_sem.at[0])
        arrived(qs_ref.at[:, pl.ds(0, 3)], out_sem.at[1])
        arrived(ks_ref.at[0, 0, pl.ds(0, 3)], out_sem.at[2])

    @pl.when(jnp.logical_not(here))
    def _():
        arrived(ks_ref, out_sem.at[0])
        arrived(qs_ref, out_sem.at[1])
        arrived(back_low_ref, out_sem.at[2])

    for i in range(2):
        arrived(arrays[i][1].at[:, pl.ds(0, 4)], halo_out.at[i])
    arrived(w_ref.at[0, :, :, pl.ds(0, GROUP)], w_out.at[0])
    arrived(w_ref.at[pl.ds(0, 6), :, :, pl.ds(0, GROUP)], w_out.at[1])
    arrived(w_ref.at[:, :, :, pl.ds(0, GROUP)], w_out.at[2])
    arrived(w_ref.at[:, :, :, pl.ds(0, 2 * GROUP)], w_out.at[3])
    down_to_sibling.wait_send()
    down_to_sibling.wait_recv()
    acc_ref[2:] = (
        (down_part_ref[half_rows(core), :] + down_got_ref[...]).astype(BF).reshape(2, 16, GROUP)
    )
    total = part_ref[half_rows(core), group_columns(x)].astype(F32)
    arrived(ra_ref, r_sem.at[1])
    for step in range(1, 8):
        total = total + ra_ref[step - 1].astype(F32)
    acc_ref[:2] = total.astype(BF).reshape(2, 16, GROUP)

    def phase_b(step):
        dy, dz = step // 4, step % 4
        return remote(
            acc_ref.at[(y + dy) % 4], rb_ref.at[y * 4 + z], r_sem.at[2], r_sem.at[3],
            device((z + dz) % 4, x, (y + dy) % 4, core),
        )

    for step in range(1, 16):
        phase_b(step).start()
    rb_ref[y * 4 + z] = acc_ref[y]
    lax.fori_loop(blocks // 2, blocks, forward, 0)
    store_mixed = pltpu.make_async_copy(mixed_ref, mixed_hbm, store_sem.at[1])
    store_mixed.start()
    arrived(rb_ref.at[pl.ds(0, 15)], r_sem.at[3])
    total = rb_ref[0].astype(F32)
    for source in range(1, 16):
        total = total + rb_ref[source].astype(F32)
    rd_ref[y // 2, y % 2] = total.astype(BF)

    def phase_d(step):
        return remote(
            rd_ref.at[y // 2, y % 2], rd_ref.at[y // 2, y % 2],
            r_sem.at[4], r_sem.at[5], y_device(step),
        )

    for step in range(1, 4):
        phase_d(step).start()
    arrived(rb_ref.at[pl.ds(0, 3)], r_sem.at[5])

    def share(tx, tc):
        return fin_ref.at[:, pl.ds(2 * tc, 2), :, group_columns(tx)]

    def phase_e(step):
        return remote(
            rd_ref, share(x, core), r_sem.at[6], e_in.at[step],
            device(z, (x + step) % CHIPS, y, core),
        )

    def pass_share(step):
        piece = share((x + CHIPS - step) % CHIPS, core)
        return remote(piece, piece, r_sem.at[7], e_in.at[0], sibling)

    for step in (2, 1, 3):
        phase_e(step).start()
    fin_ref[:, pl.ds(2 * core, 2), :, group_columns(x)] = rd_ref[...]
    pass_share(0).start()
    for step in (1, 3, 2):
        arrived(share((x + CHIPS - step) % CHIPS, core), e_in.at[step])
        pass_share(step).start()
    arrived(fin_ref.at[:, pl.ds(2 * (1 - core), 2)], e_in.at[0])
    store_grads = pltpu.make_async_copy(fin_ref, grads_hbm, store_sem.at[2])
    store_grads.start()
    arrived(ra_ref, r_sem.at[0])
    arrived(rb_ref.at[pl.ds(0, 15)], r_sem.at[2])
    arrived(rb_ref.at[pl.ds(0, 3)], r_sem.at[4])
    arrived(rb_ref.at[pl.ds(0, 12)], r_sem.at[6])
    arrived(rb_ref, r_sem.at[7])
    store_back.wait()
    store_mixed.wait()
    store_grads.wait()


def deliver_kernel(
    mixed_hbm, back_hbm, grads_hbm, mixed_out, back_out, grad_up_out, grad_down_out,
    held_ref, grads_ref, wide_ref, take_sem, put_sem,
):
    takes = [pltpu.make_async_copy(grads_hbm, grads_ref, take_sem.at[0])]
    puts = []
    for f in range(2):
        for n, (src, dst) in enumerate(((mixed_hbm, mixed_out), (back_hbm, back_out))):
            at = 1 + 2 * f + n
            takes.append(pltpu.make_async_copy(src.at[f], held_ref.at[n, f], take_sem.at[at]))
            puts.append(pltpu.make_async_copy(held_ref.at[n, f], dst.at[f], put_sem.at[at]))
    for copy in takes:
        copy.start()
    for n, dst in enumerate((grad_up_out, grad_down_out)):
        if n == 0:
            takes[0].wait()
        wide_ref[n] = grads_ref[n].astype(F32).reshape(RANK, WIDTH)
        copy = pltpu.make_async_copy(wide_ref.at[n], dst, put_sem.at[5 * n])
        copy.start()
        puts.append(copy)
    for take, put in zip(takes[1:], puts[:4]):
        take.wait()
        put.start()
    for copy in puts:
        copy.wait()


def per_device(
    queries, keys, values, head_window_radius, output_weight, adapter_down_weight, adapter_up_weight,
    output_gradient,
):
    factor = ADAPTER_SCALE / math.sqrt(GRID * GRID * COLS)
    smem = pl.BlockSpec(memory_space=pltpu.SMEM)
    hbm = pl.BlockSpec(memory_space=pl.ANY)
    block = jax.ShapeDtypeStruct((2, COLS, WIDTH), BF)
    dma = pltpu.SemaphoreType.DMA
    small = jax.ShapeDtypeStruct((RANK, WIDTH), F32)
    mixed, back, grads = pl.pallas_call(
        functools.partial(step_kernel, factor),
        out_shape=(block, block, jax.ShapeDtypeStruct((2, 4, 16, WIDTH), BF)),
        in_specs=[smem, hbm, hbm, hbm, hbm, hbm, hbm, hbm],
        out_specs=(hbm,) * 3,
        scratch_shapes=[
            pltpu.VMEM((2, COLS, WIDTH), BF),
            pltpu.VMEM((2, COLS, WIDTH), BF),
            pltpu.VMEM((GROUP_HEADS, 4, 2, COLS, HEAD_DIM), BF),
            pltpu.VMEM((GROUP_HEADS, 6, 4, COLS, HEAD_DIM), BF),
            pltpu.VMEM((GROUP_HEADS, 6, 4, COLS, HEAD_DIM), BF),
            pltpu.VMEM((GROUP_HEADS, 4, 2, COLS, HEAD_DIM), BF),
            pltpu.VMEM((8, 2, COLS, WIDTH), BF),
            pltpu.VMEM((2, COLS, WIDTH), BF),
            pltpu.VMEM((2, COLS, WIDTH), BF),
            pltpu.VMEM((RANK, WIDTH), BF),
            pltpu.VMEM((7, 32, GROUP), BF),
            pltpu.VMEM((4, 16, GROUP), BF),
            pltpu.VMEM((16, 16, GROUP), BF),
            pltpu.VMEM((2, 2, 16, GROUP), BF),
            pltpu.VMEM((2, 4, 16, WIDTH), BF),
            pltpu.VMEM((RANK, WIDTH), BF),
            pltpu.VMEM((RANK, WIDTH), BF),
            pltpu.VMEM((COLS, 2 * RANK), BF),
            pltpu.VMEM((2, 2, COLS, 2 * RANK), BF),
            pltpu.VMEM((4, 2, RANK, COLS), BF),
            pltpu.VMEM((RANK, GROUP), F32),
            pltpu.VMEM((32, GROUP), F32),
            dma((5,)), dma((3,)), dma((3, GROUP_HEADS)), dma((2,)), dma((2, GROUP_HEADS, 2)),
            dma((2,)), dma((2,)),
            dma((4,)), dma((2,)), dma((2, 3)), dma((2, 4)), dma((1,)), dma((8,)), dma((4,)), dma((3,)),
        ],
        compiler_params=pltpu.CompilerParams(
            collective_id=0, has_side_effects=True, vmem_limit_bytes=57 * 2**20
        ),
        cost_estimate=pl.CostEstimate(
            flops=14_000_000_000, bytes_accessed=100_000_000, transcendentals=7_000_000
        ),
        name="training_step",
    )(
        head_window_radius.T, queries, keys, values, output_weight,
        output_gradient.reshape(2, COLS, WIDTH), adapter_down_weight.T, adapter_up_weight,
    )
    mixed, back, grad_up, grad_down = pl.pallas_call(
        deliver_kernel,
        out_shape=(block, block, small, small),
        in_specs=[hbm] * 3,
        out_specs=(hbm,) * 4,
        scratch_shapes=[
            pltpu.VMEM((2, 2, COLS, WIDTH), BF),
            pltpu.VMEM((2, 4, 16, WIDTH), BF),
            pltpu.VMEM((2, RANK, WIDTH), F32),
            dma((5,)),
            dma((6,)),
        ],
        compiler_params=pltpu.CompilerParams(vmem_limit_bytes=60 * 2**20),
        name="deliver",
    )(mixed, back, grads)
    shape = (2, 1, COLS, WIDTH)
    return mixed.reshape(shape), back.reshape(shape), grad_up, grad_down.T


def solution(mesh):
    tokens = P("tm", "height", None, None)
    return jax.shard_map(
        per_device,
        mesh=mesh,
        in_specs=(tokens, tokens, tokens, P(), P("height", None), P(), P(), tokens),
        out_specs=(tokens, tokens, P(), P()),
        check_vma=False,
    )
```

time: 183 us -> 121 us (0.66)
  Pallas kernels: 173 us -> 120 us
  local copies, waits for them, and re-layouts: 9.16 us -> 0 us
    pallas_call x1, Pallas kernels: 173 us -> 117 us  [per_device(): pl.pallas_call(functools.partial(step_kernel, factor), out_shape=(block,...]
    unnamed x8 -> x0, local copies, waits for them, and re-layouts: 6.61 us -> none
    pallas_call x0 -> x1, Pallas kernels: none -> 3.36 us  [per_device(): pl.pallas_call(deliver_kernel, out_shape=(block, block, small, small), in...]
    transpose x1 -> x0, local copies, waits for them, and re-layouts: 2.55 us -> none  [per_device(): return (mixed.reshape(shape), back.reshape(shape), grads[0], grads[1].T)]
where the time goes in v3:
time: 121 us
  Pallas kernels  120 us (99%)
    pallas_call x1, Pallas kernels, per_device(): pl.pallas_call(functools.partial(step_kernel, factor), out_shape=(block,...  117 us
    pallas_call x1, Pallas kernels, per_device(): pl.pallas_call(deliver_kernel, out_shape=(block, block, small, small), in...  3.36 us

profile of v3, /device:TPU:1, one launch (start us, length us, event | category | flops | bytes accessed | tf_op | source)
XLA Modules:
  0.0 121.1 jit_solution(9273330857208135808)
XLA Ops:
  0.6 116.9 %training_step.1 = (bf16[2,160,2560]{2,1,0:T(8,128)(2,1)}, bf16[2,160,2560]{2,1,0:T(8,128)(2,1)}, bf16[2,4,16,2560]{3,2,1,0:T(8,128)(2,1)}) custom-call(s32[3,20]{1,0:T(4,128)} %bitcast.15, bf16[2,1,160,2560]{3,2,1,0:T(8,128)(2,1)} %q_hbm.1, bf16[2,1,160,2560]{3,2,1,0:T(8,128)(2,1)} %k_hbm.1, bf16[2,1,160,2560]{3,2,1,0:T(8,128)(2,1)} %v_hbm.1, ...), custom_call_target="tpu_custom_call" | custom-call | flops 14000000000 | bytes 100000000 | tf_op jit(solution)/shard_map/training_step/pallas_call | solution.py:630
  117.5 3.4 %deliver.1 = (bf16[2,160,2560]{2,1,0:T(8,128)(2,1)}, bf16[2,160,2560]{2,1,0:T(8,128)(2,1)}, f32[64,2560]{1,0:T(8,128)}, f32[64,2560]{1,0:T(8,128)}) custom-call(bf16[2,160,2560]{2,1,0:T(8,128)(2,1)} %get-tuple-element.11.mixed_hbm, bf16[2,160,2560]{2,1,0:T(8,128)(2,1)} %get-tuple-element.12.back_hbm, bf16[2,4,16,2560]{3,2,1,0:T(8,128)(2,1)} %get-tuple-element.13.grads_hbm), custom_call_target="tpu_custom_call" | custom-call | tf_op jit(solution)/shard_map/deliver/pallas_call | solution.py:673

commit v4 on v3

--- a/solution.py
+++ b/solution.py
@@ -111,7 +111,7 @@
     mixed_hbm, back_hbm, grads_hbm,
     mixed_ref, back_ref,
     qs_ref, ks_ref, vs_ref, os_ref, w_ref, g_ref, att_ref,
-    part_ref, ra_ref, acc_ref, rb_ref, rd_ref, fin_ref,
+    part_ref, ra_ref, acc_ref, rb_ref, rd_ref, rounded_ref, fin_ref,
     down_ref, up_ref, own_back_ref, back_low_ref, back_turned_ref, down_part_ref, down_got_ref,
     load_sem, out_sem, in_sem, halo_out, halo_in, o_in, p_sem,
     w_out, wx_in, wy_in, wz_in, ws_in, r_sem, e_in, store_sem,
@@ -251,9 +251,13 @@
             piece, slot, out_sem.at[1], o_in.at[0], device(z, frames * 2 + core, y, row)
         )
 
-    def start_back(j):
-        for n in (2, 3, 1):
-            give_back(j, n)[2].start()
+    def start_back(j, near=True, far=True):
+        if far:
+            give_back(j, 2)[2].start()
+            give_back(j, 3)[2].start()
+        if not near:
+            return
+        give_back(j, 1)[2].start()
         piece, slot, copy = give_back(j, 0)
 
         @pl.when(here)
@@ -344,6 +348,65 @@
     down_to_sibling = remote(
         down_part_ref.at[half_rows(1 - core)], down_got_ref, p_sem.at[0], p_sem.at[1], sibling
     )
+
+    def start_sum(a):
+        for step in range(1, 16):
+            sum_copy(a, step).start()
+        rb_ref[a, y * 4 + z] = acc_ref[a, y]
+
+    def sum_copy(a, step):
+        dy, dz = step // 4, step % 4
+        return remote(
+            acc_ref.at[a, (y + dy) % 4], rb_ref.at[a, y * 4 + z], r_sem.at[a, 0], r_sem.at[a, 1],
+            device((z + dz) % 4, x, (y + dy) % 4, core),
+        )
+
+    def round_y(a, step):
+        return remote(
+            rd_ref.at[a, y], rd_ref.at[a, y], r_sem.at[a, 2], r_sem.at[a, 3], y_device(step)
+        )
+
+    def finish_sum(a):
+        arrived(rb_ref.at[a, pl.ds(0, 15)], r_sem.at[a, 1])
+        total = rb_ref[a, 0]
+        for source in range(1, 16):
+            total = total + rb_ref[a, source]
+        rd_ref[a, y] = total
+        for step in range(1, 4):
+            round_y(a, step).start()
+
+    def share(a, tx, tc):
+        return fin_ref.at[a, half_rows(tc), group_columns(tx)]
+
+    def round_x(a, step):
+        return remote(
+            rounded_ref.at[a], share(a, x, core), r_sem.at[a, 4], e_in.at[a, step],
+            device(z, (x + step) % CHIPS, y, core),
+        )
+
+    def pass_share(a, step):
+        piece = share(a, (x + CHIPS - step) % CHIPS, core)
+        return remote(piece, piece, r_sem.at[a, 5], e_in.at[a, 0], sibling)
+
+    def start_round(a):
+        arrived(rb_ref.at[a, pl.ds(0, 3)], r_sem.at[a, 3])
+        rounded_ref[a] = rd_ref[a].reshape(32, GROUP).astype(BF)
+        for step in (2, 1, 3):
+            round_x(a, step).start()
+        fin_ref[a, half_rows(core), group_columns(x)] = rounded_ref[a]
+        pass_share(a, 0).start()
+
+    def pass_round(a):
+        for step in (1, 3, 2):
+            arrived(share(a, (x + CHIPS - step) % CHIPS, core), e_in.at[a, step])
+            pass_share(a, step).start()
+
+    def finish_round(a):
+        arrived(fin_ref.at[a, half_rows(1 - core)], e_in.at[a, 0])
+        arrived(rb_ref.at[a, pl.ds(0, 15)], r_sem.at[a, 0])
+        arrived(rb_ref.at[a, pl.ds(0, 3)], r_sem.at[a, 2])
+        arrived(fin_ref.at[a, pl.ds(0, 32), pl.ds(0, 3 * GROUP)], r_sem.at[a, 4])
+        arrived(fin_ref.at[a, pl.ds(0, 32)], r_sem.at[a, 5])
 
     K, V, Q = 0, 1, 2
     for copy in load_weight:
@@ -399,6 +462,7 @@
                 frame = 2 * pair + n
                 back_turned_ref[frame, row] = turned[n * RANK : (n + 1) * RANK]
     await_head(0)
+    spread_weight(3)
     weight_x(2).wait_recv()
     start_y(2, 0, (1, 3))
     weight_sibling(2, 0).start()
@@ -410,7 +474,7 @@
     start_halos(2)
     await_head(1)
     start_y(2, 0, (2,))
-    spread_weight(3)
+    spread_weight(2)
     take_z(0)
     attend_frames(1, 0, 4)
     start_back(1)
@@ -420,7 +484,6 @@
     start_halos(3)
     await_head(2)
     start_y(2, 1, (1, 3))
-    spread_weight(2)
     take_z(1)
     attend_frames(2, 0, 4)
     start_back(2)
@@ -440,8 +503,11 @@
         take_y(2, n)
     take_z(2)
     await_head(4)
-    attend_frames(4, 0, 4)
-    start_back(4)
+    far_frames = 2 * (1 - xh)
+    attend_frames(4, far_frames, far_frames + 2)
+    start_back(4, near=False)
+    attend_frames(4, 2 - far_frames, 4 - far_frames)
+    start_back(4, far=False)
     add_down(4)
     down_to_sibling.start()
 
@@ -472,9 +538,10 @@
         return carry
 
     arrived(w_ref.at[:, 1 - core], ws_in.at[0])
-    lax.fori_loop(0, CHIPS, backward, 0)
-    store_back = pltpu.make_async_copy(back_ref, back_hbm, store_sem.at[0])
-    store_back.start()
+    lax.fori_loop(0, 1, backward, 0)
+    down_to_sibling.wait_recv()
+    acc_ref[1] = (down_part_ref[half_rows(core), :] + down_got_ref[...]).reshape(4, 8, GROUP)
+    start_sum(1)
 
     arrived(att_ref, o_in.at[0])
     low = lax.dot_general(
@@ -491,7 +558,7 @@
         tx, tc, target = ring_device(step)
         return remote(
             part_ref.at[half_rows(tc), group_columns(tx)], ra_ref.at[step - 1],
-            r_sem.at[0], r_sem.at[1], target,
+            p_sem.at[2], p_sem.at[3], target,
         )
 
     for step in range(1, 8):
@@ -518,76 +585,38 @@
     arrived(w_ref.at[:, :, :, pl.ds(0, GROUP)], w_out.at[2])
     arrived(w_ref.at[:, :, :, pl.ds(0, 2 * GROUP)], w_out.at[3])
     down_to_sibling.wait_send()
-    down_to_sibling.wait_recv()
-    acc_ref[2:] = (
-        (down_part_ref[half_rows(core), :] + down_got_ref[...]).astype(BF).reshape(2, 16, GROUP)
-    )
     total = part_ref[half_rows(core), group_columns(x)].astype(F32)
-    arrived(ra_ref, r_sem.at[1])
+    arrived(ra_ref, p_sem.at[3])
     for step in range(1, 8):
         total = total + ra_ref[step - 1].astype(F32)
-    acc_ref[:2] = total.astype(BF).reshape(2, 16, GROUP)
-
-    def phase_b(step):
-        dy, dz = step // 4, step % 4
-        return remote(
-            acc_ref.at[(y + dy) % 4], rb_ref.at[y * 4 + z], r_sem.at[2], r_sem.at[3],
-            device((z + dz) % 4, x, (y + dy) % 4, core),
-        )
-
-    for step in range(1, 16):
-        phase_b(step).start()
-    rb_ref[y * 4 + z] = acc_ref[y]
+    acc_ref[0] = total.reshape(4, 8, GROUP)
+    start_sum(0)
+    finish_sum(1)
     lax.fori_loop(blocks // 2, blocks, forward, 0)
     store_mixed = pltpu.make_async_copy(mixed_ref, mixed_hbm, store_sem.at[1])
     store_mixed.start()
-    arrived(rb_ref.at[pl.ds(0, 15)], r_sem.at[3])
-    total = rb_ref[0].astype(F32)
-    for source in range(1, 16):
-        total = total + rb_ref[source].astype(F32)
-    rd_ref[y // 2, y % 2] = total.astype(BF)
-
-    def phase_d(step):
-        return remote(
-            rd_ref.at[y // 2, y % 2], rd_ref.at[y // 2, y % 2],
-            r_sem.at[4], r_sem.at[5], y_device(step),
-        )
-
-    for step in range(1, 4):
-        phase_d(step).start()
-    arrived(rb_ref.at[pl.ds(0, 3)], r_sem.at[5])
-
-    def share(tx, tc):
-        return fin_ref.at[:, pl.ds(2 * tc, 2), :, group_columns(tx)]
-
-    def phase_e(step):
-        return remote(
-            rd_ref, share(x, core), r_sem.at[6], e_in.at[step],
-            device(z, (x + step) % CHIPS, y, core),
-        )
-
-    def pass_share(step):
-        piece = share((x + CHIPS - step) % CHIPS, core)
-        return remote(piece, piece, r_sem.at[7], e_in.at[0], sibling)
-
-    for step in (2, 1, 3):
-        phase_e(step).start()
-    fin_ref[:, pl.ds(2 * core, 2), :, group_columns(x)] = rd_ref[...]
-    pass_share(0).start()
-    for step in (1, 3, 2):
-        arrived(share((x + CHIPS - step) % CHIPS, core), e_in.at[step])
-        pass_share(step).start()
-    arrived(fin_ref.at[:, pl.ds(2 * (1 - core), 2)], e_in.at[0])
-    store_grads = pltpu.make_async_copy(fin_ref, grads_hbm, store_sem.at[2])
-    store_grads.start()
-    arrived(ra_ref, r_sem.at[0])
-    arrived(rb_ref.at[pl.ds(0, 15)], r_sem.at[2])
-    arrived(rb_ref.at[pl.ds(0, 3)], r_sem.at[4])
-    arrived(rb_ref.at[pl.ds(0, 12)], r_sem.at[6])
-    arrived(rb_ref, r_sem.at[7])
+    lax.fori_loop(1, 2, backward, 0)
+    finish_sum(0)
+    start_round(1)
+    lax.fori_loop(2, 3, backward, 0)
+    start_round(0)
+    pass_round(1)
+    lax.fori_loop(3, CHIPS, backward, 0)
+    store_back = pltpu.make_async_copy(back_ref, back_hbm, store_sem.at[0])
+    store_back.start()
+    store_grads = [
+        pltpu.make_async_copy(fin_ref.at[a], grads_hbm.at[a], store_sem.at[2 + a]) for a in range(2)
+    ]
+    pass_round(0)
+    finish_round(1)
+    store_grads[1].start()
+    finish_round(0)
+    store_grads[0].start()
+    arrived(ra_ref, p_sem.at[2])
     store_back.wait()
     store_mixed.wait()
-    store_grads.wait()
+    store_grads[1].wait()
+    store_grads[0].wait()
 
 
 def deliver_kernel(
@@ -598,19 +627,22 @@
     puts = []
     for f in range(2):
         for n, (src, dst) in enumerate(((mixed_hbm, mixed_out), (back_hbm, back_out))):
-            at = 1 + 2 * f + n
-            takes.append(pltpu.make_async_copy(src.at[f], held_ref.at[n, f], take_sem.at[at]))
-            puts.append(pltpu.make_async_copy(held_ref.at[n, f], dst.at[f], put_sem.at[at]))
+            for half in range(2):
+                at = 2 + 4 * f + 2 * n + half
+                rows = pl.ds(half * HALF, HALF)
+                held = held_ref.at[n, f, rows]
+                takes.append(pltpu.make_async_copy(src.at[f, rows], held, take_sem.at[at]))
+                puts.append(pltpu.make_async_copy(held, dst.at[f, rows], put_sem.at[at]))
     for copy in takes:
         copy.start()
     for n, dst in enumerate((grad_up_out, grad_down_out)):
         if n == 0:
             takes[0].wait()
-        wide_ref[n] = grads_ref[n].astype(F32).reshape(RANK, WIDTH)
-        copy = pltpu.make_async_copy(wide_ref.at[n], dst, put_sem.at[5 * n])
+        wide_ref[n] = grads_ref[n].astype(F32)
+        copy = pltpu.make_async_copy(wide_ref.at[n], dst, put_sem.at[n])
         copy.start()
         puts.append(copy)
-    for take, put in zip(takes[1:], puts[:4]):
+    for take, put in zip(takes[1:], puts[:8]):
         take.wait()
         put.start()
     for copy in puts:
@@ -629,7 +661,7 @@
     small = jax.ShapeDtypeStruct((RANK, WIDTH), F32)
     mixed, back, grads = pl.pallas_call(
         functools.partial(step_kernel, factor),
-        out_shape=(block, block, jax.ShapeDtypeStruct((2, 4, 16, WIDTH), BF)),
+        out_shape=(block, block, jax.ShapeDtypeStruct((2, RANK, WIDTH), BF)),
         in_specs=[smem, hbm, hbm, hbm, hbm, hbm, hbm, hbm],
         out_specs=(hbm,) * 3,
         scratch_shapes=[
@@ -644,10 +676,11 @@
             pltpu.VMEM((2, COLS, WIDTH), BF),
             pltpu.VMEM((RANK, WIDTH), BF),
             pltpu.VMEM((7, 32, GROUP), BF),
-            pltpu.VMEM((4, 16, GROUP), BF),
-            pltpu.VMEM((16, 16, GROUP), BF),
-            pltpu.VMEM((2, 2, 16, GROUP), BF),
-            pltpu.VMEM((2, 4, 16, WIDTH), BF),
+            pltpu.VMEM((2, 4, 8, GROUP), F32),
+            pltpu.VMEM((2, 16, 8, GROUP), F32),
+            pltpu.VMEM((2, 4, 8, GROUP), F32),
+            pltpu.VMEM((2, 32, GROUP), BF),
+            pltpu.VMEM((2, RANK, WIDTH), BF),
             pltpu.VMEM((RANK, WIDTH), BF),
             pltpu.VMEM((RANK, WIDTH), BF),
             pltpu.VMEM((COLS, 2 * RANK), BF),
@@ -656,8 +689,8 @@
             pltpu.VMEM((RANK, GROUP), F32),
             pltpu.VMEM((32, GROUP), F32),
             dma((5,)), dma((3,)), dma((3, GROUP_HEADS)), dma((2,)), dma((2, GROUP_HEADS, 2)),
-            dma((2,)), dma((2,)),
-            dma((4,)), dma((2,)), dma((2, 3)), dma((2, 4)), dma((1,)), dma((8,)), dma((4,)), dma((3,)),
+            dma((2,)), dma((4,)),
+            dma((4,)), dma((2,)), dma((2, 3)), dma((2, 4)), dma((1,)), dma((2, 6)), dma((2, 4)), dma((4,)),
         ],
         compiler_params=pltpu.CompilerParams(
             collective_id=0, has_side_effects=True, vmem_limit_bytes=57 * 2**20
@@ -677,10 +710,10 @@
         out_specs=(hbm,) * 4,
         scratch_shapes=[
             pltpu.VMEM((2, 2, COLS, WIDTH), BF),
-            pltpu.VMEM((2, 4, 16, WIDTH), BF),
+            pltpu.VMEM((2, RANK, WIDTH), BF),
             pltpu.VMEM((2, RANK, WIDTH), F32),
-            dma((5,)),
-            dma((6,)),
+            dma((10,)),
+            dma((10,)),
         ],
         compiler_params=pltpu.CompilerParams(vmem_limit_bytes=60 * 2**20),
         name="deliver",

time: 121 us -> 118 us (0.975)
  Pallas kernels: 120 us -> 117 us
    pallas_call x1, Pallas kernels: 117 us -> 113 us  [per_device(): pl.pallas_call(functools.partial(step_kernel, factor), out_shape=(block,...]
where the time goes in v4:
time: 118 us
  Pallas kernels  117 us (99%)
    pallas_call x1, Pallas kernels, per_device(): pl.pallas_call(functools.partial(step_kernel, factor), out_shape=(block,...  113 us
    pallas_call x1, Pallas kernels, per_device(): pl.pallas_call(deliver_kernel, out_shape=(block, block, small, small), in...  3.44 us

profile of v4, /device:TPU:1, one launch (start us, length us, event | category | flops | bytes accessed | tf_op | source)
XLA Modules:
  0.0 117.6 jit_solution(8038770955075058072)
XLA Ops:
  0.6 113.3 %training_step.1 = (bf16[2,160,2560]{2,1,0:T(8,128)(2,1)}, bf16[2,160,2560]{2,1,0:T(8,128)(2,1)}, bf16[2,64,2560]{2,1,0:T(8,128)(2,1)}) custom-call(s32[3,20]{1,0:T(4,128)} %bitcast.15, bf16[2,1,160,2560]{3,2,1,0:T(8,128)(2,1)} %q_hbm.1, bf16[2,1,160,2560]{3,2,1,0:T(8,128)(2,1)} %k_hbm.1, bf16[2,1,160,2560]{3,2,1,0:T(8,128)(2,1)} %v_hbm.1, ...), custom_call_target="tpu_custom_call" | custom-call | flops 14000000000 | bytes 100000000 | tf_op jit(solution)/shard_map/training_step/pallas_call | solution.py:662
  114.0 3.4 %deliver.1 = (bf16[2,160,2560]{2,1,0:T(8,128)(2,1)}, bf16[2,160,2560]{2,1,0:T(8,128)(2,1)}, f32[64,2560]{1,0:T(8,128)}, f32[64,2560]{1,0:T(8,128)}) custom-call(bf16[2,160,2560]{2,1,0:T(8,128)(2,1)} %get-tuple-element.11.mixed_hbm, bf16[2,160,2560]{2,1,0:T(8,128)(2,1)} %get-tuple-element.12.back_hbm, bf16[2,64,2560]{2,1,0:T(8,128)(2,1)} %get-tuple-element.13.grads_hbm), custom_call_target="tpu_custom_call" | custom-call | tf_op jit(solution)/shard_map/deliver/pallas_call | solution.py:706

commit v5 on v4

--- a/solution.py
+++ b/solution.py
@@ -229,11 +229,13 @@
             arrived(arrays[i][1].at[j, pl.ds(0, 3)], halo_in.at[i, j, 1])
         landed(2, j)
 
-    def attend_frames(j, first, last):
+    def attend_frames(j, first, last, midway=None):
         head = x * GROUP_HEADS + j
         radii = [radius_ref[n, head] for n in range(3)]
 
         def one(f, carry):
+            if midway is not None:
+                pl.when(f == 2)(midway)
             for half in range(2):
                 attend(
                     j, f, half, radii, z * 4 + f, y * 4 + core * 2, qs_ref, ks_ref, vs_ref, os_ref
@@ -276,13 +278,13 @@
             2 * ((y + n) % 4) + (xl + part) % 2, core, :, group_columns((z + quarter) % 4)
         ]
 
-    def weight_x(quarter):
-        piece = weight_shard(quarter, 0, 0)
-        other = (xh + quarter // 2) % 2 * 2 + 1 - xl
-        return remote(
-            piece, piece, w_out.at[0], wx_in.at[quarter // 2],
-            device(z, other, y, core),
-        )
+    weight_x = remote(
+        weight_shard(0, 0, 0), weight_shard(0, 0, 0), w_out.at[0], wx_in.at[0],
+        device(z, (xh + core) % 2 * 2 + 1 - xl, y, core),
+    )
+    weight_across = remote(
+        weight_shard(0, 0, 1), weight_shard(0, 0, 1), w_out.at[0], wx_in.at[1], z_device(2)
+    )
 
     def weight_y(quarter, step, part):
         piece = weight_shard(quarter, 0, part)
@@ -292,12 +294,8 @@
             y_device(step),
         )
 
-    def weight_z_shard(way, part):
-        piece = weight_shard(0, 0, part)
-        return remote(piece, piece, w_out.at[2], wz_in.at[way, 0], (up, down)[way])
-
-    def weight_z(way, n):
-        piece = weight_piece(0, n, core)
+    def weight_z(way, n, part):
+        piece = weight_shard(0, n, part)
         return remote(piece, piece, w_out.at[2], wz_in.at[way, n], (up, down)[way])
 
     def weight_sibling(quarter, n):
@@ -308,18 +306,13 @@
         for step in steps:
             weight_y(quarter, step, part).start()
 
-    def start_z_shard(part):
+    def start_z(n, part):
         for way in range(2):
-            weight_z_shard(way, part).start()
+            weight_z(way, n, part).start()
 
     def take_y(quarter, n):
         arrived(weight_piece(quarter, n, core), wy_in.at[quarter // 2, n - 1])
         weight_sibling(quarter, n).start()
-
-    def spread_weight(n):
-        take_y(0, n)
-        weight_z(0, n).start()
-        weight_z(1, n).start()
 
     def take_z(n):
         for way, quarter in ((0, 1), (1, 3)):
@@ -411,12 +404,11 @@
     K, V, Q = 0, 1, 2
     for copy in load_weight:
         copy.wait()
-    weight_x(0).start()
+    weight_x.start()
     start_y(0, 0)
-    start_z_shard(0)
+    start_z(0, 0)
     give(K, 0)
     give(V, 0)
-    weight_x(2).start()
     load_gradient.wait()
     load_up.wait()
     load_down.wait()
@@ -445,14 +437,15 @@
         (K, 3), (V, 3), (Q, 2), (K, 4), (V, 4), (Q, 3), (Q, 4),
     ):
         give(i, j)
-    weight_x(0).wait_recv()
+    weight_x.wait_recv()
     start_y(0, 1)
-    start_z_shard(1)
+    start_z(0, 1)
     weight_sibling(0, 0).start()
 
     start_halos(0)
     start_corners(0)
-    spread_weight(1)
+    take_y(0, 1)
+    start_z(1, 0)
     start_halos(1)
     arrived(back_low_ref, o_in.at[1])
     for pair in range(2):
@@ -462,46 +455,45 @@
                 frame = 2 * pair + n
                 back_turned_ref[frame, row] = turned[n * RANK : (n + 1) * RANK]
     await_head(0)
-    spread_weight(3)
-    weight_x(2).wait_recv()
+    start_z(1, 1)
     start_y(2, 0, (1, 3))
-    weight_sibling(2, 0).start()
-    attend_frames(0, 0, 4)
+    attend_frames(0, 0, 4, functools.partial(start_corners, 1))
     start_back(0)
     add_down(0)
-    start_corners(1)
 
     start_halos(2)
     await_head(1)
     start_y(2, 0, (2,))
-    spread_weight(2)
+    weight_across.start()
     take_z(0)
-    attend_frames(1, 0, 4)
+    attend_frames(1, 0, 4, functools.partial(start_corners, 2))
     start_back(1)
     add_down(1)
-    start_corners(2)
 
     start_halos(3)
     await_head(2)
+    arrived(weight_shard(2, 0, 1), wx_in.at[1])
+    weight_sibling(2, 0).start()
     start_y(2, 1, (1, 3))
+    take_y(0, 3)
+    start_z(3, 0)
     take_z(1)
-    attend_frames(2, 0, 4)
+    attend_frames(2, 0, 4, functools.partial(start_corners, 3))
     start_back(2)
     add_down(2)
-    start_corners(3)
 
     start_halos(4)
     await_head(3)
     start_y(2, 1, (2,))
-    take_z(3)
-    attend_frames(3, 0, 2)
-    start_corners(4)
-    attend_frames(3, 2, 4)
+    start_z(3, 1)
+    take_y(0, 2)
+    start_z(2, 0)
+    start_z(2, 1)
+    attend_frames(3, 0, 4, functools.partial(start_corners, 4))
     start_back(3)
     add_down(3)
     for n in range(1, 4):
         take_y(2, n)
-    take_z(2)
     await_head(4)
     far_frames = 2 * (1 - xh)
     attend_frames(4, far_frames, far_frames + 2)
@@ -510,6 +502,8 @@
     start_back(4, far=False)
     add_down(4)
     down_to_sibling.start()
+    take_z(3)
+    take_z(2)
 
     step_width = 256
 
@@ -537,8 +531,6 @@
         )
         return carry
 
-    arrived(w_ref.at[:, 1 - core], ws_in.at[0])
-    lax.fori_loop(0, 1, backward, 0)
     down_to_sibling.wait_recv()
     acc_ref[1] = (down_part_ref[half_rows(core), :] + down_got_ref[...]).reshape(4, 8, GROUP)
     start_sum(1)
@@ -565,6 +557,7 @@
         phase_a(step).start()
 
     blocks = WIDTH // step_width
+    arrived(w_ref.at[:, 1 - core], ws_in.at[0])
     lax.fori_loop(0, blocks // 2, forward, 0)
     @pl.when(here)
     def _():
@@ -595,7 +588,7 @@
     lax.fori_loop(blocks // 2, blocks, forward, 0)
     store_mixed = pltpu.make_async_copy(mixed_ref, mixed_hbm, store_sem.at[1])
     store_mixed.start()
-    lax.fori_loop(1, 2, backward, 0)
+    lax.fori_loop(0, 2, backward, 0)
     finish_sum(0)
     start_round(1)
     lax.fori_loop(2, 3, backward, 0)

time: 118 us -> 115 us (0.975)
  Pallas kernels: 117 us -> 114 us
    pallas_call x1, Pallas kernels: 113 us -> 111 us  [per_device(): pl.pallas_call(functools.partial(step_kernel, factor), out_shape=(block,...]
where the time goes in v5:
time: 115 us
  Pallas kernels  114 us (99%)
    pallas_call x1, Pallas kernels, per_device(): pl.pallas_call(functools.partial(step_kernel, factor), out_shape=(block,...  111 us
    pallas_call x1, Pallas kernels, per_device(): pl.pallas_call(deliver_kernel, out_shape=(block, block, small, small), in...  3.44 us

profile of v5, /device:TPU:1, one launch (start us, length us, event | category | flops | bytes accessed | tf_op | source)
XLA Modules:
  0.0 115.3 jit_solution(4094404118791562612)
XLA Ops:
  0.6 111.0 %training_step.1 = (bf16[2,160,2560]{2,1,0:T(8,128)(2,1)}, bf16[2,160,2560]{2,1,0:T(8,128)(2,1)}, bf16[2,64,2560]{2,1,0:T(8,128)(2,1)}) custom-call(s32[3,20]{1,0:T(4,128)} %bitcast.15, bf16[2,1,160,2560]{3,2,1,0:T(8,128)(2,1)} %q_hbm.1, bf16[2,1,160,2560]{3,2,1,0:T(8,128)(2,1)} %k_hbm.1, bf16[2,1,160,2560]{3,2,1,0:T(8,128)(2,1)} %v_hbm.1, ...), custom_call_target="tpu_custom_call" | custom-call | flops 14000000000 | bytes 100000000 | tf_op jit(solution)/shard_map/training_step/pallas_call | solution.py:655
  111.7 3.4 %deliver.1 = (bf16[2,160,2560]{2,1,0:T(8,128)(2,1)}, bf16[2,160,2560]{2,1,0:T(8,128)(2,1)}, f32[64,2560]{1,0:T(8,128)}, f32[64,2560]{1,0:T(8,128)}) custom-call(bf16[2,160,2560]{2,1,0:T(8,128)(2,1)} %get-tuple-element.11.mixed_hbm, bf16[2,160,2560]{2,1,0:T(8,128)(2,1)} %get-tuple-element.12.back_hbm, bf16[2,64,2560]{2,1,0:T(8,128)(2,1)} %get-tuple-element.13.grads_hbm), custom_call_target="tpu_custom_call" | custom-call | tf_op jit(solution)/shard_map/deliver/pallas_call | solution.py:699

commit v6 on v5

--- a/solution.py
+++ b/solution.py
@@ -539,22 +539,26 @@
     low = lax.dot_general(
         att_ref[...].reshape(tokens, WIDTH), down_ref[...], contract_last, preferred_element_type=F32
     ).astype(BF)
-    part_ref[...] = (
-        factor
-        * lax.dot_general(
-            low, g_ref[...].reshape(tokens, WIDTH), contract_first, preferred_element_type=F32
-        )
-    ).astype(BF)
-
-    def phase_a(step):
-        tx, tc, target = ring_device(step)
+    low_turned = low.astype(F32).T.astype(BF)
+
+    def phase_a(dx, dc):
+        tx, tc = (x + dx) % CHIPS, (core + dc) % 2
         return remote(
-            part_ref.at[half_rows(tc), group_columns(tx)], ra_ref.at[step - 1],
-            p_sem.at[2], p_sem.at[3], target,
-        )
-
-    for step in range(1, 8):
-        phase_a(step).start()
+            part_ref.at[half_rows(tc), group_columns(tx)], ra_ref.at[2 * dx + dc - 1],
+            p_sem.at[2], p_sem.at[3], device(z, tx, y, tc),
+        )
+
+    for dx in (2, 1, 3, 0):
+        columns = group_columns((x + dx) % CHIPS)
+        part_ref[:, columns] = (
+            factor
+            * jnp.dot(
+                low_turned, g_ref[:, :, columns].reshape(tokens, GROUP), preferred_element_type=F32
+            )
+        ).astype(BF)
+        for dc in range(2):
+            if dx + dc > 0:
+                phase_a(dx, dc).start()
 
     blocks = WIDTH // step_width
     arrived(w_ref.at[:, 1 - core], ws_in.at[0])

time: 115 us -> 115 us (level)
  no operation moved by 1% of the time
where the time goes in v6:
time: 115 us
  Pallas kernels  114 us (99%)
    pallas_call x1, Pallas kernels, per_device(): pl.pallas_call(functools.partial(step_kernel, factor), out_shape=(block,...  111 us
    pallas_call x1, Pallas kernels, per_device(): pl.pallas_call(deliver_kernel, out_shape=(block, block, small, small), in...  3.44 us

profile of v6, /device:TPU:1, one launch (start us, length us, event | category | flops | bytes accessed | tf_op | source)
XLA Modules:
  0.0 114.8 jit_solution(8546528792537795521)
XLA Ops:
  0.6 110.5 %training_step.1 = (bf16[2,160,2560]{2,1,0:T(8,128)(2,1)}, bf16[2,160,2560]{2,1,0:T(8,128)(2,1)}, bf16[2,64,2560]{2,1,0:T(8,128)(2,1)}) custom-call(s32[3,20]{1,0:T(4,128)} %bitcast.15, bf16[2,1,160,2560]{3,2,1,0:T(8,128)(2,1)} %q_hbm.1, bf16[2,1,160,2560]{3,2,1,0:T(8,128)(2,1)} %k_hbm.1, bf16[2,1,160,2560]{3,2,1,0:T(8,128)(2,1)} %v_hbm.1, ...), custom_call_target="tpu_custom_call" | custom-call | flops 14000000000 | bytes 100000000 | tf_op jit(solution)/shard_map/training_step/pallas_call | solution.py:659
  111.2 3.4 %deliver.1 = (bf16[2,160,2560]{2,1,0:T(8,128)(2,1)}, bf16[2,160,2560]{2,1,0:T(8,128)(2,1)}, f32[64,2560]{1,0:T(8,128)}, f32[64,2560]{1,0:T(8,128)}) custom-call(bf16[2,160,2560]{2,1,0:T(8,128)(2,1)} %get-tuple-element.11.mixed_hbm, bf16[2,160,2560]{2,1,0:T(8,128)(2,1)} %get-tuple-element.12.back_hbm, bf16[2,64,2560]{2,1,0:T(8,128)(2,1)} %get-tuple-element.13.grads_hbm), custom_call_target="tpu_custom_call" | custom-call | tf_op jit(solution)/shard_map/deliver/pallas_call | solution.py:703
